TPU v7x, 32 devices: a whole 2x2x4 slice. The times are simulated.
32 devices in a mesh: dp: 8 (over z, x), blk: 4 (over y, core).
Axes of the slice: x: 2, y: 2, z: 4, core: 2. Of those that a mesh axis runs over, the one named last changes fastest.
Arguments:
- tokens: bfloat16 [62976, 512], P(('dp', 'blk')), may hold values from -6 to 6
- sides: int32 [32], P(('dp', 'blk')), may hold values from 5 to 9, as said below
- cpe_weight: bfloat16 [9, 512], replicated, may hold values from -2 to 2
- cpe_bias: bfloat16 [512], replicated, may hold values from -2 to 2
- norm1_gain: bfloat16 [512], replicated, may hold values from 0.5 to 1.5
- norm1_shift: bfloat16 [512], replicated, may hold values from -2 to 2
- w_qkv: bfloat16 [512, 1536], replicated, may hold values from -0.375 to 0.375
- query_bias: bfloat16 [512], replicated, may hold values from -2 to 2
- value_bias: bfloat16 [512], replicated, may hold values from -2 to 2
- crpe_small: bfloat16 [9, 128], replicated, may hold values from -1 to 1
- crpe_middle: bfloat16 [25, 192], replicated, may hold values from -0.625 to 0.625
- crpe_large: bfloat16 [49, 192], replicated, may hold values from -0.4375 to 0.4375
- crpe_bias: bfloat16 [512], replicated, may hold values from -2 to 2
- w_proj: bfloat16 [512, 512], replicated, may hold values from -0.375 to 0.375
- proj_bias: bfloat16 [512], replicated, may hold values from -2 to 2
- norm2_gain: bfloat16 [512], replicated, may hold values from 0.5 to 1.5
- norm2_shift: bfloat16 [512], replicated, may hold values from -2 to 2
- w_fc1: bfloat16 [512, 2048], P(None, 'blk'), may hold values from -0.25 to 0.25
- fc1_bias: bfloat16 [2048], P('blk'), may hold values from -2 to 2
- w_fc2: bfloat16 [2048, 512], P('blk'), may hold values from -0.1875 to 0.1875
- fc2_bias: bfloat16 [512], replicated, may hold values from -2 to 2
- cotangent: bfloat16 [62976, 512], P(('dp', 'blk')), may hold values from -6 to 6
Outputs:
- output: bfloat16 [62976, 512], P(('dp', 'blk'))
- grad_tokens: bfloat16 [62976, 512], P(('dp', 'blk'))
- grad_cpe_weight: float32 [9, 512], replicated
- grad_cpe_bias: float32 [512], replicated
- grad_norm1_gain: float32 [512], replicated
- grad_norm1_shift: float32 [512], replicated
- grad_w_qkv: float32 [512, 1536], replicated
- grad_query_bias: float32 [512], replicated
- grad_value_bias: float32 [512], replicated
- grad_crpe_small: float32 [9, 128], replicated
- grad_crpe_middle: float32 [25, 192], replicated
- grad_crpe_large: float32 [49, 192], replicated
- grad_crpe_bias: float32 [512], replicated
- grad_w_proj: float32 [512, 512], replicated
- grad_proj_bias: float32 [512], replicated
- grad_norm2_gain: float32 [512], replicated
- grad_norm2_shift: float32 [512], replicated
- grad_w_fc1: float32 [512, 2048], P(None, 'blk')
- grad_fc1_bias: float32 [2048], P('blk')
- grad_w_fc2: float32 [2048, 512], P('blk')
- grad_fc2_bias: float32 [512], replicated
Inputs may be any that keep to these rules, and one draw needn't show every extreme that they name: Every image of batch group g has a patch grid of sides[g] x sides[g] cells, sides[g] odd; in every draw some group has 9 and some group 5.
All inputs are finite; a program needn't handle non-finite values.
Results may differ from a plain program's by a relative error of at most 0.014.
Values may be sent and summed in bfloat16 or wider, within the bound.
No kernel may reach another device: no remote copies, remote signals or barrier semaphores. Data moves between devices by JAX's collectives and lax.ppermute only.
A program may use at most 512 MiB of HBM per device.

v0:
```python
import functools
import math

import jax
import jax.numpy as jnp
from jax import lax
from jax.experimental import pallas as pl
from jax.experimental.pallas import tpu as pltpu
from jax.sharding import PartitionSpec as P

HEADS = 8
GRID = 9
CELLS = GRID * GRID
SLOT = CELLS + 1
LANES = 128
EPSILON = 1e-6
SLOT_PAD = 96
TILE = 256
BAND = 128
MLP_TILE = 1024
KERNEL_SIZES = (3, 5, 7, 7)
PIECE = 256
VMEM_BYTES = 62 * 1024 * 1024

F32 = jnp.float32
BF16 = jnp.bfloat16

SMALL_ROWS = (56, 58, 49, 50, 64, 65, 66)
CPE_B, GAIN1, SHIFT1, QUERY_B, VALUE_B, CRPE_B, PROJ_B = range(7)
GAIN2, SHIFT2, FC2_B = range(3)


def dot(left, right):
    return lax.dot_general(left, right, (((1,), (0,)), ((), ())), preferred_element_type=F32)


def dot_nt(left, right):
    return lax.dot_general(left, right, (((1,), (1,)), ((), ())), preferred_element_type=F32)


def dot_tn(left, right):
    return lax.dot_general(left, right, (((0,), (0,)), ((), ())), preferred_element_type=F32)


class Copies:
    def __init__(self, sems):
        self.sems, self.count, self.open = sems, 0, []

    def start(self, source, target):
        assert self.count < self.sems.shape[0]
        copy = pltpu.make_async_copy(source, target, self.sems.at[self.count])
        self.count += 1
        copy.start()
        self.open.append(copy)
        return copy

    def wait(self, copy):
        copy.wait()
        self.open = [other for other in self.open if other is not copy]

    def finish(self):
        for copy in self.open:
            copy.wait()


def loop(count, body, unroll=1):
    def step(index, carry):
        body(index)
        return carry

    lax.fori_loop(0, count, step, 0, unroll=unroll)


def rows_at(start, count, multiple=8):
    return pl.ds(pl.multiple_of(start, multiple), count)


def lanes_of(block):
    return slice(block * LANES, (block + 1) * LANES)


def fold_rows(values):
    count, lanes = values.shape
    return jnp.sum(values.reshape(count // 8, 8, lanes), 0)


def fill_mask(side, mask_ref, images):
    mask_ref[SLOT * images :, :] = jnp.zeros_like(mask_ref[SLOT * images :, :])

    def body(slot):
        row = slot // GRID
        col = slot - row * GRID
        inside = (slot == CELLS) | ((row < side) & (col < side))
        level = jnp.where(inside, 1.0, 0.0).astype(F32)
        mask_ref[rows_at(slot * images, images), :] = jnp.full((images, LANES), level, F32)

    loop(SLOT, body, unroll=2)


def spread(rows_ref, blocks_ref, blocks):
    total = rows_ref.shape[0]

    def body(step):
        at = rows_at(step * 48, 48, 16)
        values = rows_ref[at, :].astype(F32)
        for block in range(blocks):
            blocks_ref[block, at, :] = values[:, lanes_of(block)]

    loop(total // 48, body)


def unspread(blocks_ref, rows_ref, blocks):
    total = rows_ref.shape[0]

    def body(step):
        at = rows_at(step * 48, 48, 16)
        values = [blocks_ref[block, at, :] for block in range(blocks)]
        rows_ref[at, :] = jnp.concatenate(values, 1).astype(BF16)

    loop(total // 48, body)


def natural_slot(slot):
    return jnp.where(slot == CELLS, 0, slot + 1)


def fill_table(vectors, table_ref):
    for row, ref in enumerate(vectors):
        table_ref[row : row + 1, :] = ref[...].astype(F32).reshape(1, -1)


def fill_taps(table, taps_ref, count, blocks):
    for tap in range(count):
        for block in range(blocks):
            taps_ref[block, tap] = jnp.broadcast_to(table[tap : tap + 1, lanes_of(block)], (8, LANES))


def centred(size):
    inset = (7 - size) // 2
    return [(a + inset) * 7 + b + inset for a in range(size) for b in range(size)]


def lane_picker(width, offset, channels):
    lane = lax.broadcasted_iota(jnp.int32, (width, channels), 0)
    channel = lax.broadcasted_iota(jnp.int32, (width, channels), 1)
    return jnp.where(channel == lane + offset, 1.0, 0.0).astype(BF16)


def assemble_taps(kernels, work_ref, table_ref):
    channels = table_ref.shape[1]
    table_ref[...] = jnp.zeros_like(table_ref)
    offset = 0
    for size, kernel_ref in zip((3, 5, 7), kernels):
        width = kernel_ref.shape[1]
        work_ref[0 : size * size, :] = dot(kernel_ref[...], lane_picker(width, offset, channels))
        for tap, place in enumerate(centred(size)):
            table_ref[place : place + 1, :] += work_ref[tap : tap + 1, :]
        offset += width


def correlate(source_ref, taps_ref, size, span, images, block, sub, emit, turned=False, beside=()):
    margin, inset = size // 2, (span - size) // 2
    beside = iter(beside)

    def load(cell):
        return source_ref[block, rows_at(cell * images + sub * 8, 8), :]

    for row in range(GRID):
        totals = [None] * GRID
        for a in range(size):
            from_row = row + a - margin
            if not 0 <= from_row < GRID:
                continue
            cells = [load(from_row * GRID + col) for col in range(GRID)]
            for b in range(size):
                tap = (a + inset) * span + b + inset
                weight = taps_ref[block, span * span - 1 - tap if turned else tap]
                for col in range(GRID):
                    from_col = col + b - margin
                    if 0 <= from_col < GRID:
                        term = cells[from_col] * weight
                        totals[col] = term if totals[col] is None else totals[col] + term
        for col in range(GRID):
            emit(row * GRID + col, totals[col])
        next(beside, None)
        next(beside, None)
    for _ in beside:
        pass


def tap_sums(grad_ref, source_ref, sums_ref, size, span, images, block, sub):
    margin, inset = size // 2, (span - size) // 2

    def load(ref, cell):
        return ref[block, rows_at(cell * images + sub * 8, 8), :]

    for a in range(size):
        totals = [None] * size
        for row in range(GRID):
            from_row = row + a - margin
            if not 0 <= from_row < GRID:
                continue
            grads = [load(grad_ref, row * GRID + col) for col in range(GRID)]
            cells = [load(source_ref, from_row * GRID + col) for col in range(GRID)]
            for b in range(size):
                part = None
                for col in range(GRID):
                    from_col = col + b - margin
                    if 0 <= from_col < GRID:
                        term = grads[col] * cells[from_col]
                        part = term if part is None else part + term
                totals[b] = part if totals[b] is None else totals[b] + part
        for b in range(size):
            tap = (a + inset) * span + b + inset
            sums_ref[block, tap] += totals[b]


def by_block(images, body, before=None, beside=None):
    subs = images // 8
    first = 0
    while first < len(KERNEL_SIZES):
        size = KERNEL_SIZES[first]
        count = 1
        while first + count < len(KERNEL_SIZES) and KERNEL_SIZES[first + count] == size:
            count += 1
        for block in range(first, first + count):
            if before is not None:
                before(block)
        last = beside is not None and first + count == len(KERNEL_SIZES)
        share = images // (count * subs)

        def step(index, first=first, size=size, last=last, share=share):
            if last:
                work = (part for one in range(share) for part in beside(index * share + one))
                body(size, first + index // subs, index % subs, work)
            else:
                body(size, first + index // subs, index % subs)

        loop(count * subs, step)
        first += count


def row_sums(value):
    high = value.astype(BF16)
    low = (value - high.astype(F32)).astype(BF16)
    return dot(jnp.concatenate([high, low], 1), jnp.ones((2 * LANES, LANES), BF16))


def row_means(blocks):
    return row_sums(sum(blocks[1:], blocks[0])) * (1.0 / (len(blocks) * LANES))


def norm_parts(blocks):
    mean = row_means(blocks)
    centered = [value - mean for value in blocks]
    inverse = lax.rsqrt(row_means([value * value for value in centered]) + EPSILON)
    return [value * inverse for value in centered], inverse


def norm_forward(source_ref, table_ref, gain_row, shift_row, normed_ref, turned_ref, parts_ref, inverse_ref, keep=None):
    blocks = source_ref.shape[0]
    gains = table_ref[gain_row : gain_row + 1, :]
    shifts = table_ref[shift_row : shift_row + 1, :]

    def body(step):
        at = rows_at(step * BAND, BAND, BAND)
        source = [source_ref[block, at, :] for block in range(blocks)]
        if keep is not None:
            keep(at, source)
        parts, inverse = norm_parts(source)
        inverse_ref[at, :] = inverse
        for block in range(blocks):
            parts_ref[block, at, :] = parts[block]
        out = [
            parts[block] * gains[:, lanes_of(block)] + shifts[:, lanes_of(block)]
            for block in range(blocks)
        ]
        normed_ref[at, :] = jnp.concatenate(out, 1).astype(BF16)

    loop(source_ref.shape[1] // BAND, body, unroll=2)
    transpose_rows(normed_ref, turned_ref)


def transpose_rows(rows_ref, turned_ref):
    width = rows_ref.shape[1]

    def body(step):
        at = rows_at(step * TILE, TILE, TILE)
        turned_ref[0:width, at] = rows_ref[at, :].T

    loop(rows_ref.shape[0] // TILE, body)


def norm_backward(parts_ref, inverse_ref, grad_at, direct_at, table_ref, gain_row, emit, blocks, total):
    gains = table_ref[gain_row : gain_row + 1, :]

    def body(step, sums):
        at = rows_at(step * BAND, BAND, BAND)
        parts, inverse = [parts_ref[block, at, :] for block in range(blocks)], inverse_ref[at, :]
        grads = [grad_at(block, at) for block in range(blocks)]
        scaled = [grads[block] * gains[:, lanes_of(block)] for block in range(blocks)]
        product = [grads[block] * parts[block] for block in range(blocks)]
        crossed = [product[block] * gains[:, lanes_of(block)] for block in range(blocks)]
        mean, cross = row_means(scaled), row_means(crossed)
        out = [
            direct_at(block, at) + inverse * (scaled[block] - mean - parts[block] * cross)
            for block in range(blocks)
        ]
        emit(at, out)
        gain_sums = [sums[0][block] + fold_rows(product[block]) for block in range(blocks)]
        shift_sums = [sums[1][block] + fold_rows(grads[block]) for block in range(blocks)]
        return (gain_sums, shift_sums)

    zero = [jnp.zeros((8, LANES), F32) for _ in range(blocks)]
    return lax.fori_loop(0, total // BAND, body, (zero, zero), unroll=2)


def total_row(parts):
    return jnp.concatenate([jnp.sum(part, 0, keepdims=True) for part in parts], 1)


def head_mask():
    row = lax.broadcasted_iota(jnp.int32, (LANES, LANES), 0)
    col = lax.broadcasted_iota(jnp.int32, (LANES, LANES), 1)
    size = LANES // 2
    return jnp.where((row < size) == (col < size), size ** (-0.5), 0.0).astype(F32)


def pack_kernel(bias_ref, fc1_ref, fc2_ref, packed_ref):
    channels = fc1_ref.shape[0]
    packed_ref[0:channels, :] = fc1_ref[...]
    packed_ref[channels : 2 * channels, :] = fc2_ref[...]
    rest = packed_ref.at[2 * channels :, :]
    rest[...] = jnp.broadcast_to(bias_ref[...].reshape(1, -1), rest.shape)


def front_kernel(
    side_ref, tokens_ref, cpe_ref, small_ref, middle_ref, large_ref, qkv_ref, proj_ref,
    cpe_bias_ref, gain_ref, shift_ref, query_bias_ref, value_bias_ref, crpe_bias_ref, proj_bias_ref,
    crpe_ref, mask_out, input_out, parts_out, inverse_out, query_out, weight_out, value_out, convolved_out, normed_t_out, context_out, attended_t_out, second_out,
    input_ref, inverse_ref, query_ref, weight_ref, value_ref, convolved_ref, normed_t_ref, context_ref, attended_t_ref,
    second_ref, position_ref, mask_ref, work_ref, normed_ref, cpe_taps_ref, crpe_taps_ref, crpe_work_ref, table_ref, sems,
):
    fill_table(
        (cpe_bias_ref, gain_ref, shift_ref, query_bias_ref, value_bias_ref, crpe_bias_ref, proj_bias_ref), table_ref
    )
    out = Copies(sems)
    rows, channels = tokens_ref.shape
    blocks = channels // LANES
    images = rows // SLOT
    padded = normed_ref.shape[0]
    held = SLOT_PAD * images
    fill_mask(side_ref[0], mask_ref, images)
    assemble_taps((small_ref, middle_ref, large_ref), crpe_work_ref, crpe_ref)
    fill_taps(cpe_ref[...].astype(F32), cpe_taps_ref, 9, blocks)
    fill_taps(crpe_ref, crpe_taps_ref, 49, blocks)
    spread(tokens_ref, work_ref, blocks)

    def arrange(slot):
        at = rows_at(slot * images, images)
        mask = mask_ref[at, :]
        for block in range(blocks):
            values = work_ref[block, pl.ds(natural_slot(slot), images, stride=SLOT), :]
            input_ref[block, at, :] = values * mask

    out.start(mask_ref, mask_out)
    loop(SLOT, arrange, unroll=2)
    for ref in (input_ref, position_ref, convolved_ref):
        ref[:, rows:padded, :] = jnp.zeros((blocks, padded - rows, LANES), F32)
    position_ref[:, CELLS * images : rows, :] = input_ref[:, CELLS * images : rows, :]
    convolved_ref[:, CELLS * images : rows, :] = jnp.zeros((blocks, images, LANES), F32)

    subs = images // 8

    def position(index):
        block, sub = index // subs, index % subs
        bias = table_row(table_ref, CPE_B, block)

        def emit(cell, total):
            at = rows_at(cell * images + sub * 8, 8)
            position_ref[block, at, :] = input_ref[block, at, :] + mask_ref[at, :] * (total + bias)

        correlate(input_ref, cpe_taps_ref, 3, 3, images, block, sub, emit)

    loop(blocks * subs, position)
    out.start(input_ref, input_out)
    norm_forward(
        position_ref, table_ref, GAIN1, SHIFT1, normed_ref, normed_t_ref, second_ref, inverse_ref
    )
    sent_parts = out.start(second_ref, parts_out)
    out.start(inverse_ref, inverse_out)
    normed_t_ref[channels:, :] = jnp.ones_like(normed_t_ref[channels:, :])
    out.start(normed_t_ref, normed_t_out)

    def project(step):
        at = rows_at(step * TILE, TILE, TILE)
        normed = normed_ref[at, :]
        mask = mask_ref[at, :]
        query = dot(normed, qkv_ref[:, :channels]) + table_ref[QUERY_B : QUERY_B + 1, :]
        for block in range(blocks):
            query_ref[block, at, :] = query[:, lanes_of(block)]
        key = dot(normed, qkv_ref[:, channels : 2 * channels])
        for block in range(blocks):
            weight_ref[block, at, :] = key[:, lanes_of(block)]
        value = dot(normed, qkv_ref[:, 2 * channels :]) + table_ref[VALUE_B : VALUE_B + 1, :]
        for block in range(blocks):
            value_ref[block, at, :] = value[:, lanes_of(block)] * mask

    loop(padded // TILE, project)
    for ref in (query_ref, value_ref):
        ref[:, padded:held, :] = jnp.zeros((blocks, held - padded, LANES), F32)
    weight_ref[:, rows:held, :] = jnp.zeros((blocks, held - rows, LANES), F32)
    out.start(query_ref, query_out)
    out.start(value_ref, value_out)

    def soften(index):
        block, sub = index // subs, index % subs
        top = None
        for slot in range(SLOT):
            at = rows_at(slot * images + sub * 8, 8)
            key = jnp.where(mask_ref[at, :] > 0, weight_ref[block, at, :], -1e30)
            top = key if top is None else jnp.maximum(top, key)
        total = None
        for slot in range(SLOT):
            at = rows_at(slot * images + sub * 8, 8)
            mask = mask_ref[at, :]
            key = jnp.where(mask > 0, weight_ref[block, at, :], -1e30)
            level = jnp.exp(key - top) * mask
            weight_ref[block, at, :] = level
            total = level if total is None else total + level
        inverse = 1.0 / total
        for slot in range(SLOT):
            at = rows_at(slot * images + sub * 8, 8)
            weight_ref[block, at, :] = weight_ref[block, at, :] * inverse

    loop(blocks * subs, soften)
    out.start(weight_ref, weight_out)
    heads = head_mask()

    def attend(image):
        at = pl.ds(image, SLOT_PAD, stride=images)
        for block in range(blocks):
            weight = weight_ref[block, at, :].astype(BF16)
            value = value_ref[block, at, :].astype(BF16)
            query = query_ref[block, at, :].astype(BF16)
            context = (dot_tn(weight, value) * heads).astype(BF16)
            context_ref[image, block] = context
            work_ref[block, at, :] = dot(query, context)
            yield

    def convolve(size, block, sub, beside=()):
        bias = table_row(table_ref, CRPE_B, block)

        def emit(cell, total):
            convolved_ref[block, rows_at(cell * images + sub * 8, 8), :] = total + bias

        correlate(value_ref, crpe_taps_ref, size, 7, images, block, sub, emit, beside=beside)

    by_block(images, convolve, beside=attend)
    out.start(convolved_ref, convolved_out)
    out.start(context_ref, context_out)
    out.wait(sent_parts)

    def finish(step):
        at = rows_at(step * TILE, TILE, TILE)
        attended = jnp.concatenate(
            [
                work_ref[block, at, :] + query_ref[block, at, :] * convolved_ref[block, at, :]
                for block in range(blocks)
            ],
            1,
        ).astype(BF16)
        attended_t_ref[:, at] = attended.T
        branch = dot(attended, proj_ref[...]) + table_ref[PROJ_B : PROJ_B + 1, :]
        for block in range(blocks):
            second_ref[block, at, :] = position_ref[block, at, :] + branch[:, lanes_of(block)]

    half = padded // TILE // 2
    loop(half, finish)
    part = slice(0, half * TILE)
    out.start(second_ref.at[:, part], second_out.at[:, part])
    loop(padded // TILE - half, lambda step: finish(step + half))
    part = slice(half * TILE, padded)
    out.start(second_ref.at[:, part], second_out.at[:, part])
    out.start(attended_t_ref, attended_t_out)
    out.finish()


def table_row(table_ref, row, block):
    return table_ref[row : row + 1, pl.ds(pl.multiple_of(block * LANES, LANES), LANES)]


def gelu_parts(value):
    level = 0.5 + 0.5 * lax.erf(value * math.sqrt(0.5))
    return level, jnp.exp2(value * value * (-0.5 / math.log(2.0))) * (1.0 / math.sqrt(2.0 * math.pi))


def mlp_kernel(
    side_ref, cot_ref, mask_ref, second_in, fc_in, gain_ref, shift_ref, fc2_bias_ref,
    result_out, grad_out, grad_fc_keep, grad_fc_send, small_ref,
    second_ref, fc_ref, grad_ref, grad_fc_ref,
    work_ref, cot_rows_ref, cot_t_ref, normed_ref, normed_t_ref, hidden_ref, pre_ref, hidden_two_ref, pre_two_ref, mlp_ref, back_ref,
    table_ref, result_ref, inverse_ref, sems,
):
    fill_table((gain_ref, shift_ref, fc2_bias_ref), table_ref)
    copies = Copies(sems)
    got_second = copies.start(second_in, second_ref)
    got_fc = copies.start(fc_in, fc_ref)
    rows, channels = cot_ref.shape
    blocks = channels // LANES
    images = rows // SLOT
    padded = normed_ref.shape[0]
    owners, _, units = fc_ref.shape
    mine, half_x, half_z = side_ref[1], side_ref[2] & 1, (side_ref[2] >> 1) & 1
    spread(cot_ref, work_ref, blocks)
    cot_rows_ref[rows:padded, :] = jnp.zeros((padded - rows, channels), BF16)

    def arrange(step, sums):
        at = rows_at(step * (2 * images), 2 * images, 16)
        mask = mask_ref[at, :]
        parts = []
        for block in range(blocks):
            pair = [
                work_ref[block, pl.ds(natural_slot(2 * step + one), images, stride=SLOT), :]
                for one in range(2)
            ]
            parts.append(jnp.concatenate(pair, 0) * mask)
        cot_rows_ref[at, :] = jnp.concatenate(parts, 1).astype(BF16)
        return [sums[block] + fold_rows(parts[block]) for block in range(blocks)]

    zero = [jnp.zeros((8, LANES), F32) for _ in range(blocks)]
    bias_sums = lax.fori_loop(0, SLOT // 2, arrange, zero)
    transpose_rows(cot_rows_ref, cot_t_ref)
    got_second.wait()
    fc2_bias = table_ref[FC2_B : FC2_B + 1, :]

    def keep(at, second):
        for block in range(blocks):
            mlp_ref[at, lanes_of(block)] = second[block] + fc2_bias[:, lanes_of(block)]

    norm_forward(
        second_ref, table_ref, GAIN2, SHIFT2, normed_ref, normed_t_ref, second_ref, inverse_ref, keep
    )
    normed_t_ref[channels:, :] = jnp.ones_like(normed_t_ref[channels:, :])
    half = units // 2
    got_fc.wait()

    full = padded // MLP_TILE
    wide = units // full
    ends = 2
    rows_half = MLP_TILE // ends

    def weights(slot, held, step):
        cols = pl.ds(pl.multiple_of(step * wide, wide), wide)
        hidden_ref, pre_ref = held
        for which, (left_ref, right_ref) in enumerate(((normed_t_ref, pre_ref), (cot_t_ref, hidden_ref))):
            grad = dot(left_ref[...], right_ref[:, cols]).astype(BF16)
            for end in range(2):
                place = ((half_x ^ which) << 1) | (half_z ^ end)
                grad_fc_ref[slot, place, 0:PIECE, cols] = grad[end * PIECE : (end + 1) * PIECE]
            if which == 0:
                grad_fc_ref[slot, (half_x << 1) | half_z, PIECE:, cols] = grad[channels:]
            yield

    def part(slot, held, before):
        owner = mine ^ ((slot >> 1) | ((slot & 1) << 1))
        hidden_ref, pre_ref = held

        def tile(step):
            beside = iter(()) if before is None else weights(slot - 1, before, step)
            for end in range(ends):
                at = rows_at(step * MLP_TILE + end * rows_half, rows_half, rows_half)
                normed = normed_ref[at, :]
                cot = cot_rows_ref[at, :]
                mlp, back = None, None
                for piece in range(2):
                    cols = slice(piece * half, (piece + 1) * half)
                    first = fc_ref[owner, 0:channels, cols]
                    second = fc_ref[owner, channels + piece * half : channels + (piece + 1) * half, :]
                    bias = fc_ref[owner, 2 * channels :, cols].astype(F32)[0:1]
                    values, grads = dot(normed, first), dot_nt(cot, second)
                    if piece == 0:
                        next(beside, None)
                    values = values + bias
                    level, density = gelu_parts(values)
                    hidden = (values * level).astype(BF16)
                    pre = (grads * (level + values * density)).astype(BF16)
                    hidden_ref[at, cols] = hidden
                    pre_ref[at, cols] = pre
                    more_mlp, more_back = dot(hidden, second), dot_nt(pre, first)
                    mlp = more_mlp if mlp is None else mlp + more_mlp
                    back = more_back if back is None else back + more_back
                if slot == 0:
                    back_ref[at, :] = back
                else:
                    back_ref[at, :] += back
                if slot < owners - 1:
                    mlp_ref[at, :] += mlp
                else:
                    result_ref[at, :] = (mlp_ref[at, :] + mlp).astype(BF16)

        loop(full, tile)

    def last_weights(step):
        for _ in weights(owners - 1, held[(owners - 1) % 2], step):
            pass

    held = (hidden_ref, pre_ref), (hidden_two_ref, pre_two_ref)
    targets = [(grad_fc_keep if slot < owners // 2 else grad_fc_send).at[slot % (owners // 2)] for slot in range(owners)]
    for slot in range(owners + 1):
        if slot < owners:
            part(slot, held[slot % 2], held[(slot - 1) % 2] if slot else None)
        else:
            loop(full, last_weights)
        if slot:
            copies.start(grad_fc_ref.at[slot - 1], targets[slot - 1])

    def grad_at(block, at):
        return back_ref[at, lanes_of(block)]

    def direct_at(block, at):
        return cot_rows_ref[at, lanes_of(block)].astype(F32)

    def emit(at, out):
        for block in range(blocks):
            grad_ref[block, at, :] = out[block]

    gain_sums, shift_sums = norm_backward(
        second_ref, inverse_ref, grad_at, direct_at, table_ref, GAIN2, emit, blocks, padded
    )
    copies.start(grad_ref, grad_out)
    copies.start(result_ref, result_out)
    small_ref[...] = jnp.zeros_like(small_ref)
    small_ref[0:1, :] = total_row(gain_sums)
    small_ref[1:2, :] = total_row(shift_sums)
    small_ref[2:3, :] = total_row(bias_sums)
    for copy in copies.open[2:]:
        copy.wait()


def result_kernel(result_ref, mask_ref, out_ref, work_ref):
    rows, channels = out_ref.shape
    blocks = channels // LANES
    images = rows // SLOT

    def arrange(step):
        at = rows_at(step * (2 * images), 2 * images, 16)
        values = result_ref[at, :].astype(F32)
        mask = mask_ref[at, :]
        for block in range(blocks):
            masked = values[:, lanes_of(block)] * mask
            for one in range(2):
                to = pl.ds(natural_slot(2 * step + one), images, stride=SLOT)
                work_ref[block, to, :] = masked[one * images : (one + 1) * images]

    loop(SLOT // 2, arrange)
    unspread(work_ref, out_ref, blocks)


def branch_kernel(
    proj_ref, grad_in, attended_t_in,
    back_out, grad_proj_ref, small_ref,
    grad_ref, attended_t_ref, back_ref, branch_ref, sems,
):
    copies = Copies(sems)
    padded, channels = branch_ref.shape
    blocks = channels // LANES
    held = back_ref.shape[1]
    half = padded // 2
    halves = slice(0, half), slice(half, padded)
    got = [copies.start(grad_in.at[:, part], grad_ref.at[:, part]) for part in halves]
    got_attended = copies.start(attended_t_in, attended_t_ref)
    back_ref[:, padded:held, :] = jnp.zeros((blocks, held - padded, LANES), F32)
    sent = [copies.start(back_ref.at[:, padded:held], back_out.at[:, padded:held])]

    total = jnp.zeros((8, channels), F32)
    step = half // 2
    for end, part in enumerate(halves):
        got[end].wait()
        for first in range(end * half, (end + 1) * half, step):
            at = slice(first, first + step)
            low = jnp.concatenate([grad_ref[block, at, :] for block in range(blocks)], 1).astype(BF16)
            branch_ref[at, :] = low
            total += fold_rows(low.astype(F32))
            back = dot_nt(low, proj_ref[...])
            for block in range(blocks):
                back_ref[block, at, :] = back[:, lanes_of(block)]
        sent.append(copies.start(back_ref.at[:, part], back_out.at[:, part]))
    got_attended.wait()
    grad_proj_ref[...] = dot(attended_t_ref[...], branch_ref[...]).astype(BF16)
    small_ref[...] = total
    for copy in sent:
        copy.wait()


def mix_kernel(
    side_ref, small_mlp_ref, small_branch_ref, crpe_ref, grad_proj_ref,
    back_in, query_in, weight_in, value_in, convolved_in, normed_t_in, context_in, mask_in,
    keep_ref, send_ref, projected_out,
    total_ref, back_ref, query_ref, weight_ref, value_ref, convolved_ref, normed_t_ref, context_ref, projected_ref,
    mask_ref, small_ref, edge_ref, turned_ref, crpe_taps_ref, sems,
):
    copies = Copies(sems)
    pairs = (back_in, back_ref), (query_in, query_ref), (convolved_in, convolved_ref)
    first = [
        [copies.start(source.at[block], target.at[block]) for source, target in pairs] for block in range(back_ref.shape[0])
    ]
    pairs = (weight_in, weight_ref), (value_in, value_ref), (context_in, context_ref), (mask_in, mask_ref)
    pairs += ((normed_t_in, normed_t_ref),)
    then = [copies.start(*pair) for pair in pairs]
    blocks, padded, _ = edge_ref.shape
    channels = blocks * LANES
    held = query_ref.shape[1]
    images = held // SLOT_PAD
    rows = images * SLOT
    subs = images // 8
    fill_taps(crpe_ref, crpe_taps_ref, 49, blocks)
    turned_ref[:, CELLS * images :, :] = jnp.zeros((blocks, padded - CELLS * images, LANES), F32)
    bias_sums = []

    def arrived(block):
        for copy in first[block]:
            copy.wait()

        def edges(step, total):
            at = rows_at(step * (9 * images), 9 * images)
            back = back_ref[block, at, :]
            edge = back * query_ref[block, at, :]
            edge_ref[block, at, :] = edge
            convolved_ref[block, at, :] = back * convolved_ref[block, at, :]
            return total + fold_rows(edge)

        bias_sums.append(lax.fori_loop(0, CELLS // 9, edges, jnp.zeros((8, LANES), F32)))

    def convolve(size, block, sub):
        def emit(cell, total):
            turned_ref[block, rows_at(cell * images + sub * 8, 8), :] = total

        correlate(edge_ref, crpe_taps_ref, size, 7, images, block, sub, emit, turned=True)

    by_block(images, convolve, arrived)
    for copy in then:
        copy.wait()
    heads = head_mask()

    def attend(image):
        at = pl.ds(image, SLOT_PAD, stride=images)
        for block in range(blocks):
            weight = weight_ref[block, at, :]
            low = weight.astype(BF16)
            value = value_ref[block, at, :].astype(BF16)
            query = query_ref[block, at, :].astype(BF16)
            back = back_ref[block, at, :].astype(BF16)
            context = context_ref[image, block]
            grad = (dot_tn(query, back) * heads).astype(BF16)
            query_ref[block, at, :] = dot_nt(back, context)
            key = dot_nt(value, grad)
            back_ref[block, at, :] = weight * (key - jnp.sum(weight * key, 0, keepdims=True))
            value_ref[block, at, :] = dot(low, grad)

    loop(images, attend, unroll=4)
    projected_ref[rows:padded, :] = jnp.zeros((padded - rows, 3 * channels), BF16)

    def gather(step):
        at = rows_at(step * (2 * images), 2 * images, 16)
        mask = mask_ref[at, :]
        parts = [[], [], []]
        for block in range(blocks):
            parts[0].append(query_ref[block, at, :] + convolved_ref[block, at, :])
            parts[1].append(back_ref[block, at, :])
            parts[2].append((value_ref[block, at, :] + turned_ref[block, at, :]) * mask)
        for which in range(3):
            cols = slice(which * channels, (which + 1) * channels)
            projected_ref[at, cols] = jnp.concatenate(parts[which], 1).astype(BF16)

    loop(SLOT // 2, gather)
    sent = copies.start(projected_ref, projected_out)
    small_ref[...] = jnp.zeros_like(small_ref)
    index = ((side_ref[1] & 1) << 2) | ((side_ref[2] & 1) << 1) | (side_ref[1] >> 1)

    def place(matrix, grad):
        for end in range(channels // PIECE):
            piece = matrix * (channels // PIECE) + end
            total_ref[piece ^ index, 0:PIECE, :] = grad[end * PIECE : (end + 1) * PIECE]

    for which in range(3):
        cols = slice(which * channels, (which + 1) * channels)
        grad = dot(normed_t_ref[...], projected_ref[:, cols])
        place(which, grad[0:channels].astype(BF16))
        small_ref[56 + which : 57 + which, :] = grad[channels : channels + 1]
    place(3, grad_proj_ref[...])
    small_ref[49:50, :] = total_row(bias_sums)
    small_ref[50:51, :] = jnp.sum(small_branch_ref[...], 0, keepdims=True)
    small_ref[64:72, :] = small_mlp_ref[...]
    for piece in range(total_ref.shape[0]):
        total_ref[piece ^ index, PIECE:, :] = small_ref[piece * 16 : (piece + 1) * 16, :].astype(BF16)
    out = [copies.start(total_ref.at[4:8], send_ref), copies.start(total_ref.at[0:4], keep_ref)]
    for copy in [sent] + out:
        copy.wait()


def taps_kernel(
    back_in, query_in, value_in,
    small_ref,
    back_ref, query_ref, value_ref, sums_ref, sems,
):
    copies = Copies(sems)
    blocks, cells, _ = back_ref.shape
    images = cells // CELLS
    part = slice(0, cells)
    pairs = (back_in, back_ref), (query_in, query_ref), (value_in, value_ref)
    got = [
        [copies.start(source.at[block, part], target.at[block]) for source, target in pairs] for block in range(blocks)
    ]
    sums_ref[...] = jnp.zeros_like(sums_ref)

    def arrived(block):
        for copy in got[block]:
            copy.wait()

        def edges(step):
            at = rows_at(step * (9 * images), 9 * images)
            back_ref[block, at, :] = back_ref[block, at, :] * query_ref[block, at, :]

        loop(CELLS // 9, edges)

    def taps(size, block, sub):
        tap_sums(back_ref, value_ref, sums_ref, size, 7, images, block, sub)

    by_block(images, taps, arrived)
    small_ref[...] = jnp.zeros_like(small_ref)
    for block in range(blocks):
        small_ref[0:49, lanes_of(block)] = jnp.sum(sums_ref[block], 1)


def norm_half(
    copies, first, base, operands, grad_out, projected_ref, parts_ref, inverse_ref, grad_ref, normed_ref, table_ref
):
    qkv_ref, gain_ref, projected_in, parts_in, inverse_in, grad_in = operands
    fill_table((gain_ref,), table_ref)
    padded, channels = normed_ref.shape
    blocks = channels // LANES
    half = padded // 2
    got_halves = [
        copies.start(projected_in.at[pl.ds(first + end * half, half)], projected_ref.at[pl.ds(end * half, half)])
        for end in range(2)
    ]
    source, target = pl.ds(first, padded), pl.ds(base, padded)
    got = [
        copies.start(parts_in.at[:, source], parts_ref),
        copies.start(inverse_in.at[source], inverse_ref),
        copies.start(grad_in.at[:, source], grad_ref.at[:, target]),
    ]

    for end in range(2):
        got_halves[end].wait()
        at = slice(end * half, (end + 1) * half)
        normed_ref[at, :] = dot_nt(projected_ref[at, :], qkv_ref[...])
    for copy in got:
        copy.wait()

    def grad_at(block, at):
        return normed_ref[at, lanes_of(block)]

    def moved(at):
        return rows_at(base + at.start, at.size, BAND)

    def direct_at(block, at):
        return grad_ref[block, moved(at), :]

    def emit_norm(at, out):
        for block in range(blocks):
            grad_ref[block, moved(at), :] = out[block]

    sums = norm_backward(parts_ref, inverse_ref, grad_at, direct_at, table_ref, 0, emit_norm, blocks, padded)
    return copies.start(grad_ref.at[:, target], grad_out), sums


def norm_first_kernel(
    qkv_ref, gain_ref, projected_in, parts_in, inverse_in, grad_in,
    grad_out, small_ref,
    projected_ref, parts_ref, inverse_ref, grad_ref, normed_ref, table_ref, sems,
):
    operands = qkv_ref, gain_ref, projected_in, parts_in, inverse_in, grad_in
    sent, (gain_sums, shift_sums) = norm_half(
        Copies(sems), 0, 0, operands, grad_out, projected_ref, parts_ref, inverse_ref, grad_ref, normed_ref,
        table_ref,
    )
    small_ref[...] = jnp.zeros_like(small_ref)
    small_ref[0:1, :] = total_row(gain_sums)
    small_ref[1:2, :] = total_row(shift_sums)
    sent.wait()


def norm_last_kernel(
    first, qkv_ref, gain_ref, projected_in, parts_in, inverse_in, grad_in, grad_first_in, input_in, small_first_ref,
    small_taps_ref,
    grad_out, small_ref,
    projected_ref, parts_ref, inverse_ref, grad_ref, normed_ref, table_ref, input_ref, sums_ref, work_ref, sems,
):
    copies = Copies(sems)
    blocks, cells, _ = input_ref.shape
    images = cells // CELLS
    subs = images // 8
    got = copies.start(grad_first_in, grad_ref.at[:, 0:first]), copies.start(input_in.at[:, 0:cells], input_ref)
    operands = qkv_ref, gain_ref, projected_in, parts_in, inverse_in, grad_in
    sent, (gain_sums, shift_sums) = norm_half(
        copies, first, first, operands, grad_out, projected_ref, parts_ref, inverse_ref, grad_ref, normed_ref,
        table_ref,
    )
    sums_ref[...] = jnp.zeros_like(sums_ref)
    work_ref[...] = jnp.zeros_like(work_ref)
    work_ref[0:56, :] = small_taps_ref[...]
    work_ref[57:58, :] = total_row(gain_sums) + small_first_ref[0:1, :]
    work_ref[58:59, :] = total_row(shift_sums) + small_first_ref[1:2, :]
    for copy in got:
        copy.wait()

    def colsum(step, sums):
        at = rows_at(step * (9 * images), 9 * images)
        return [sums[block] + fold_rows(grad_ref[block, at, :]) for block in range(blocks)]

    zero = [jnp.zeros((8, LANES), F32) for _ in range(blocks)]
    work_ref[56:57, :] = total_row(lax.fori_loop(0, GRID, colsum, zero))

    def taps(index):
        tap_sums(grad_ref, input_ref, sums_ref, 3, 3, images, index // subs, index % subs)

    loop(blocks * subs, taps)
    for block in range(blocks):
        work_ref[64:73, lanes_of(block)] = jnp.sum(sums_ref[block], 1)
    small_ref[...] = work_ref[...].astype(BF16)
    sent.wait()


def back_kernel(
    mask_ref, cpe_ref, first_in, second_in,
    tokens_ref,
    grad_ref, work_ref, result_ref, taps_ref, sems,
):
    copies = Copies(sems)
    half = first_in.shape[1]
    got = copies.start(first_in, grad_ref.at[:, 0:half]), copies.start(second_in, grad_ref.at[:, half : 2 * half])
    rows, channels = tokens_ref.shape
    blocks = channels // LANES
    images = rows // SLOT
    subs = images // 8
    fill_taps(cpe_ref[...].astype(F32), taps_ref, 9, blocks)
    for copy in got:
        copy.wait()

    def convolve(index):
        block, sub = index // subs, index % subs

        def emit(cell, total):
            at = rows_at(cell * images + sub * 8, 8)
            result_ref[block, at, :] = (grad_ref[block, at, :] + total) * mask_ref[at, :]

        correlate(grad_ref, taps_ref, 3, 3, images, block, sub, emit, turned=True)

    loop(blocks * subs, convolve)
    result_ref[:, CELLS * images : rows, :] = grad_ref[:, CELLS * images : rows, :]

    def arrange(slot):
        at = rows_at(slot * images, images)
        for block in range(blocks):
            work_ref[block, pl.ds(natural_slot(slot), images, stride=SLOT), :] = result_ref[block, at, :]

    loop(SLOT, arrange, unroll=2)
    unspread(work_ref, tokens_ref, blocks)


def finish_fc_kernel(
    side_ref, first_ref, second_ref, third_ref, fourth_ref,
    fc1_ref, fc2_ref, bias_ref,
    held_ref,
):
    index = ((side_ref[2] & 1) << 1) | ((side_ref[2] >> 1) & 1)
    for place, piece in enumerate((first_ref, second_ref, third_ref, fourth_ref)):
        held_ref[place ^ index] = piece[...]
    for end in range(2):
        fc1_ref[end * PIECE : (end + 1) * PIECE, :] = held_ref[end, 0:PIECE, :].astype(F32)
        fc2_ref[:, end * PIECE : (end + 1) * PIECE] = held_ref[2 + end, 0:PIECE, :].astype(F32).T
    bias_ref[...] = held_ref[0, PIECE:, :].astype(F32)[0:1].reshape(bias_ref.shape)


def finish_small_kernel(
    small_ref,
    cpe_ref, cpe_bias_ref, gain_ref, shift_ref, crpe_small_ref, crpe_middle_ref, crpe_large_ref,
    work_ref,
):
    small = small_ref[...]
    work_ref[...] = small.astype(F32)
    cpe_ref[...] = work_ref[64:73, :]
    for row, ref in enumerate((cpe_bias_ref, gain_ref, shift_ref)):
        ref[...] = work_ref[56 + row : 57 + row, :].reshape(ref.shape)
    channels = small.shape[1]
    offset = 0
    for size, ref in zip((3, 5, 7), (crpe_small_ref, crpe_middle_ref, crpe_large_ref)):
        width = ref.shape[1]
        taps = dot_nt(small, lane_picker(width, offset, channels))
        for tap, place in enumerate(centred(size)):
            ref[tap : tap + 1, :] = taps[place : place + 1, :]
        offset += width


def finish_kernel(side_ref, *refs):
    pieces, (qkv_out, proj_out), rows = refs[:8], refs[8:10], refs[10:-5]
    held_ref, small_ref, qkv_ref, proj_ref, sems = refs[-5:]
    copies = Copies(sems)
    index = ((side_ref[1] & 1) << 2) | ((side_ref[2] & 1) << 1) | (side_ref[1] >> 1)
    for place, piece in enumerate(pieces):
        held_ref[place ^ index] = piece[...]
    channels = proj_ref.shape[1]
    for piece in range(8):
        matrix, end = piece // 2, piece % 2
        at = slice(end * PIECE, (end + 1) * PIECE)
        cols = slice(matrix * channels, (matrix + 1) * channels)
        values = held_ref[piece, 0:PIECE, :].astype(F32)
        if matrix < 3:
            qkv_ref[at, cols] = values
            copies.start(qkv_ref.at[at, cols], qkv_out.at[at, cols])
        else:
            proj_ref[at, :] = values
            copies.start(proj_ref.at[at], proj_out.at[at])
        small_ref[piece * 16 : (piece + 1) * 16, :] = held_ref[piece, PIECE:, :].astype(F32)
    for row, ref in zip(SMALL_ROWS, rows):
        ref[...] = small_ref[row : row + 1, :].reshape(ref.shape)
    copies.finish()


def add(*terms):
    return sum(term.astype(F32) for term in terms).astype(BF16)


def exchange(values, across_dp, across_blk):
    owners, parts = lax.axis_size("blk"), lax.axis_size("dp")
    flip = across_dp * owners + across_blk
    return lax.ppermute(values, ("dp", "blk"), [(at, at ^ flip) for at in range(parts * owners)])


def together(*values):
    return lax.optimization_barrier(values)


def shape(dims, dtype):
    return jax.ShapeDtypeStruct(dims, dtype)


def call(body, outs, scratch, cost, *operands):
    vmem, smem, hbm = (pl.BlockSpec(memory_space=space) for space in (pltpu.VMEM, pltpu.SMEM, pl.ANY))

    def place(value):
        return hbm if isinstance(value, Held) else smem if value.dtype == jnp.int32 else vmem

    def plain(values):
        return [value.array if isinstance(value, Held) else value for value in values]

    return pl.pallas_call(
        body,
        out_shape=plain(outs),
        in_specs=[place(value) for value in operands],
        out_specs=[place(value) for value in outs],
        scratch_shapes=[
            pltpu.SemaphoreType.DMA((item,)) if isinstance(item, int) else pltpu.VMEM(*item) for item in scratch
        ],
        compiler_params=pltpu.CompilerParams(vmem_limit_bytes=VMEM_BYTES),
        cost_estimate=pl.CostEstimate(flops=cost, bytes_accessed=cost // 1000, transcendentals=0),
    )(*plain(operands))


class Held:
    def __init__(self, array):
        self.array = array


def shards(
    tokens, sides, cpe_weight, cpe_bias, norm1_gain, norm1_shift, w_qkv, query_bias, value_bias,
    crpe_small, crpe_middle, crpe_large, crpe_bias, w_proj, proj_bias, norm2_gain, norm2_shift,
    w_fc1, fc1_bias, w_fc2, fc2_bias, cotangent,
):
    rows, channels = tokens.shape
    blocks = channels // LANES
    images = rows // SLOT
    padded = -(-rows // TILE) * TILE
    held = SLOT_PAD * images
    units = w_fc1.shape[1]
    owners = lax.axis_size("blk")

    (packed,) = call(
        pack_kernel, [shape((2 * channels + 16, units), BF16)], [], 1_000_000, fc1_bias, w_fc1, w_fc2
    )
    fc_all = lax.all_gather(packed, "blk", axis=0, tiled=False)
    scalars = jnp.stack([sides[0], lax.axis_index("blk"), lax.axis_index("dp")]).astype(jnp.int32)
    block_rows = (blocks, padded, LANES)
    block_held = (blocks, held, LANES)
    block_cells = (blocks, CELLS * images, LANES)
    contexts = (images, blocks, LANES, LANES), BF16
    front = [
        (block_rows, F32), (block_rows, F32), ((padded, LANES), F32), (block_held, F32), (block_held, F32), (block_held, F32),
        (block_rows, F32), ((channels + 16, padded), BF16), contexts, ((channels, padded), BF16), (block_rows, F32),
    ]
    crpe, mask, inputs, parts, inverse, query, weight, value, convolved, normed_t, context, attended_t, second = call(
        front_kernel,
        [shape((56, channels), F32), Held(shape((padded, LANES), F32))] + [Held(shape(*item)) for item in front],
        front[:1] + front[2:] + [
            (block_rows, F32), ((padded, LANES), F32), (block_held, F32), ((padded, channels), BF16),
            ((blocks, 9, 8, LANES), F32), ((blocks, 49, 8, LANES), F32), ((56, channels), F32), ((8, channels), F32), 13,
        ],
        40_000_000_000,
        scalars, tokens, cpe_weight, crpe_small, crpe_middle, crpe_large, w_qkv, w_proj,
        cpe_bias, norm1_gain, norm1_shift, query_bias, value_bias, crpe_bias, proj_bias,
    )
    pieces = (owners // 2, 4, PIECE + 16, units)
    result, grad_second, fc_keep, fc_send, small_mlp = call(
        mlp_kernel,
        [
            Held(shape((padded, channels), BF16)), Held(shape(block_rows, F32)), Held(shape(pieces, BF16)),
            Held(shape(pieces, BF16)),
            shape((8, channels), F32),
        ],
        [
            (block_rows, F32), (fc_all.shape, BF16), (block_rows, F32),
            ((owners, 4, PIECE + 16, units), BF16),
            ((blocks, rows, LANES), F32),
            ((padded, channels), BF16), ((channels, padded), BF16),
            ((padded, channels), BF16), ((channels + 16, padded), BF16),
            ((padded, units), BF16), ((padded, units), BF16), ((padded, units), BF16), ((padded, units), BF16),
            ((padded, channels), F32), ((padded, channels), F32), ((8, channels), F32), ((padded, channels), BF16), ((padded, LANES), F32), 4 + owners,
        ],
        60_000_000_000,
        scalars, cotangent, mask, Held(second), Held(fc_all), norm2_gain, norm2_shift, fc2_bias,
    )
    fc_far = exchange(fc_send, 0, 1)
    back, grad_proj, small_branch = call(
        branch_kernel,
        [Held(shape(block_held, F32)), shape((channels, channels), BF16), shape((8, channels), F32)],
        [(block_rows, F32), ((channels, padded), BF16), (block_held, F32), ((padded, channels), BF16), 6],
        10_000_000_000,
        w_proj, Held(grad_second), Held(attended_t),
    )

    def half_of(side, end):
        part = slice(2 * end, 2 * end + 2)
        return add(fc_keep[side, part], fc_far[side, part])

    back, fc_y, fc_x, fc_yx, fc_own = together(back, half_of(1, 0), half_of(0, 1), half_of(1, 1), half_of(0, 0))
    fc_far = exchange(fc_y, 0, 2), exchange(fc_x, 1, 0), exchange(fc_yx, 1, 2)
    total_keep, total_send, projected = call(
        mix_kernel,
        [Held(shape((4, PIECE + 16, channels), BF16))] * 2 + [Held(shape((padded, 3 * channels), BF16))],
        [
            ((8, PIECE + 16, channels), BF16),
            (block_held, F32), (block_held, F32), (block_held, F32), (block_held, F32), (block_rows, F32),
            ((channels + 16, padded), BF16), contexts, ((padded, 3 * channels), BF16),
            ((padded, LANES), F32), ((128, channels), F32), (block_rows, F32), (block_rows, F32),
            ((blocks, 49, 8, LANES), F32), 8 + 3 * blocks,
        ],
        50_000_000_000,
        scalars, small_mlp, small_branch, crpe, grad_proj,
        Held(back), Held(query), Held(weight), Held(value), Held(convolved), Held(normed_t), Held(context),
        Held(mask),
    )
    projected, total_keep, total_send, *fc_far = together(projected, total_keep, total_send, *fc_far)
    total_far = exchange(total_send, 0, 1)
    bits = [1 << bit for bit in range(1, lax.axis_size("dp").bit_length() - 1)]
    fc_bits = [bit for bit in bits if bit > 2]

    def end_of(end):
        return add(fc_own[end], *(far[end] for far in fc_far))

    fc_other, fc_own = end_of(1), end_of(0)
    sums = [add(total_keep[piece], total_far[piece]) for piece in range(4)]
    projected, fc_own, fc_other, *sums = together(projected, fc_own, fc_other, *sums)
    fc_far = exchange(fc_other, 2, 0)
    total_far = exchange(sums[1], 0, 2), exchange(sums[2], 1, 0), exchange(sums[3], 1, 2)
    block_half = (blocks, padded // 2, LANES)
    norm_outs = [Held(shape(block_half, F32)), shape((8, channels), F32)]
    norm_scratch = [((padded // 2, 3 * channels), BF16), (block_half, F32), ((padded // 2, LANES), F32)]
    norm_more = [((padded // 2, channels), F32), ((8, channels), F32)]
    grad_first, small_first = call(
        norm_first_kernel, norm_outs, norm_scratch + [(block_half, F32)] + norm_more + [6], 8_000_000_000,
        w_qkv, norm1_gain, Held(projected), Held(parts), Held(inverse), Held(grad_second),
    )
    back, grad_first, fc_own, own = together(back, grad_first, add(fc_own, fc_far), add(sums[0], *total_far))
    total_far = exchange(own, bits[0], 0)
    fc_far = exchange(fc_own, fc_bits[0], 0)
    (small_taps,) = call(
        taps_kernel,
        [shape((56, channels), F32)],
        [(block_cells, F32), (block_cells, F32), (block_cells, F32), ((blocks, 49, 8, LANES), F32), 3 * blocks],
        15_000_000_000,
        Held(back), Held(query), Held(value),
    )
    fc_own = add(fc_own, fc_far)
    for bit in fc_bits[1:]:
        fc_own = add(fc_own, exchange(fc_own, bit, 0))
    projected, small_taps, fc_own, own = together(projected, small_taps, fc_own, add(own, total_far))
    total_far = exchange(own, bits[1], 0)
    fc_other, fc_third = exchange(fc_own, 2, 0), exchange(fc_own, 1, 0)
    grad_last, small_back = call(
        functools.partial(norm_last_kernel, padded // 2),
        [norm_outs[0], shape((80, channels), BF16)],
        norm_scratch + [(block_rows, F32)] + norm_more
        + [(block_cells, F32), ((blocks, 9, 8, LANES), F32), ((80, channels), F32), 8],
        12_000_000_000,
        w_qkv, norm1_gain, Held(projected), Held(parts), Held(inverse), Held(grad_second), Held(grad_first), Held(inputs),
        small_first, small_taps,
    )
    own = add(own, total_far)
    for bit in bits[2:]:
        own = add(own, exchange(own, bit, 0))
    grad_last, small_back, result, fc_other, fc_third, own = together(
        grad_last, small_back, result, fc_other, fc_third, own
    )
    near = [own, exchange(own, 0, 2), exchange(own, 1, 0), exchange(own, 1, 2)]
    small_far, fc_fourth = exchange(small_back, 0, 1), exchange(fc_other, 1, 0)
    (output,) = call(
        result_kernel, [shape((rows, channels), BF16)], [((blocks, rows, LANES), F32)], 1_000_000,
        result, mask,
    )
    output, small, small_far, fc_fourth = together(output, small_back, small_far, fc_fourth)
    small, grad_last = together(add(small, small_far), grad_last)
    small_far = exchange(small, 0, 2)
    (grad_tokens,) = call(
        back_kernel,
        [shape((rows, channels), BF16)],
        [
            (block_rows, F32), ((blocks, rows, LANES), F32),
            (block_rows, F32), ((blocks, 9, 8, LANES), F32), 2,
        ],
        1_000_000,
        mask, cpe_weight, Held(grad_first), Held(grad_last),
    )
    grad_tokens, small, small_far, *near = together(grad_tokens, small, small_far, *near)
    total_pieces = near + [exchange(piece, 0, 1) for piece in near]
    small = add(small, small_far)
    small_far = exchange(small, 1, 0)
    small, fc_own = together(small, fc_own)
    fc1, fc2, fc1_sums = call(
        finish_fc_kernel,
        [shape((channels, units), F32), shape((units, channels), F32), shape((units,), F32)],
        [((4, PIECE + 16, units), BF16)],
        1_000_000,
        scalars, fc_own, fc_other, fc_third, fc_fourth,
    )
    fc1, small, small_far, *total_pieces = together(fc1, small, small_far, *total_pieces)
    small = add(small, small_far)
    small_far = [exchange(small, flip, 0) for flip in (bits[0], bits[1], bits[0] | bits[1])]
    row = shape((channels,), F32)
    grad_qkv, grad_proj, query_sums, value_sums, crpe_sums, proj_sums, gain_two, shift_two, fc2_sums = call(
        finish_kernel,
        [Held(shape((channels, 3 * channels), F32)), Held(shape((channels, channels), F32))] + [row] * len(SMALL_ROWS),
        [
            ((8, PIECE + 16, channels), BF16), ((128, channels), F32),
            ((channels, 3 * channels), F32), ((channels, channels), F32), 8,
        ],
        1_000_000,
        scalars, *total_pieces,
    )
    grad_qkv, small, *small_far = together(grad_qkv, small, *small_far)
    terms = [term.astype(F32) for term in (small, *small_far)]
    small = ((terms[0] + terms[1]) + (terms[2] + terms[3])).astype(BF16)
    for bit in bits[2:]:
        small = add(small, exchange(small, bit, 0))
    cpe, cpe_sums, gain_one, shift_one, taps_small, taps_middle, taps_large = call(
        finish_small_kernel,
        [
            shape(cpe_weight.shape, F32), row, row, row,
            shape(crpe_small.shape, F32), shape(crpe_middle.shape, F32), shape(crpe_large.shape, F32),
        ],
        [((80, channels), F32)],
        1_000_000,
        small,
    )
    return (
        output, grad_tokens, cpe, cpe_sums, gain_one, shift_one, grad_qkv, query_sums, value_sums,
        taps_small, taps_middle, taps_large, crpe_sums, grad_proj, proj_sums, gain_two, shift_two,
        fc1, fc1_sums, fc2, fc2_sums,
    )


def solution(mesh):
    split, whole = P(("dp", "blk"), None), P()
    fc1, fc1_bias, fc2 = P(None, "blk"), P("blk"), P("blk", None)
    return jax.shard_map(
        shards,
        mesh=mesh,
        in_specs=(split, P(("dp", "blk"))) + (whole,) * 15 + (fc1, fc1_bias, fc2, whole, split),
        out_specs=(split, split) + (whole,) * 15 + (fc1, fc1_bias, fc2, whole),
        check_vma=False,
    )
```

profile of v0, /device:TPU:0, one launch (start us, length us, event | category | flops | bytes accessed | tf_op | source)
XLA Modules:
  0.0 248.2 jit_solution(11887122287698497735)
XLA Ops:
  7.2 2.3 shard_map.374
  10.8 33.2 %shard_map.373 = (f32[56,512]{1,0:T(8,128)}, f32[2048,128]{1,0:T(8,128)}, f32[4,2048,128]{2,1,0:T(8,128)}, f32[4,2048,128]{2,1,0:T(8,128)}, f32[2048,128]{1,0:T(...) custom-call(s32[3]{0:T(128)} %pad_add_fusion.side_ref, ...), custom_call_target="tpu_custom_call" | custom-call | flops 40000000000 | bytes 40000000 | tf_op jit(solution)/shard_map/pallas_call | solution.py:1059
  44.0 3.8 %all-gather.3.cloned.1.call-done = bf16[4160,512]{1,0:T(8,128)(2,1)} async-done(((bf16[1040,512]{1,0:T(8,128)(2,1)}), bf16[4160,512]{1,0:T(8,128)(2,1)}) %all-gather.3.cloned.1.call-update) | async-done | bytes 4259856 | tf_op jit(solution)/shard_map/all_gather | solution.py:1093
  47.8 44.5 %shard_map.375 = (bf16[2048,512]{1,0:T(8,128)(2,1)}, f32[4,2048,128]{2,1,0:T(8,128)}, bf16[2,4,272,512]{3,2,1,0:T(8,128)(2,1)}, bf16[2,4,272,512]{3,2,1,0:T(8,128)(2,1)}, f32[8,512]{1,0:T(8,128)}) custom-call(s32[3]{0:T(128)} %pad_add_fusion.side_ref, bf16[1968,512]{1,0:T(8,128)(2,1)} %cot_ref.1, f32[2048,128]{1,0:T(8,128)} %get-tuple-element.131.mask_ref.mask_in, ...), custom_call_target="tpu_custom_call" | custom-call | flops 60000002048 | bytes 60000000 | tf_op jit(solution)/shard_map/pallas_call | solution.py:1059
  92.6 6.5 %shard_map.376 = (f32[4,2304,128]{2,1,0:T(8,128)}, bf16[512,512]{1,0:T(8,128)(2,1)}, f32[8,512]{1,0:T(8,128)}) custom-call(bf16[512,512]{1,0:T(8,128)(2,1)} %proj_ref.3, f32[4,2048,128]{2,1,0:T(8,128)} %get-tuple-element.134.grad_in, bf16[512,2048]{1,0:T(8,128)(2,1)} %get-tuple-element.135.attended_t_in), custom_call_target="tpu_custom_call" | custom-call | flops 10000000000 | bytes 10000000 | tf_op jit(solution)/shard_map/pallas_call | solution.py:1059
  99.1 3.7 %fusion.3 = (bf16[2,272,512]{2,1,0:T(8,128)(2,1)S(1)}, bf16[2,272,512]{2,1,0:T(8,128)(2,1)S(1)}, bf16[2,272,512]{2,1,0:T(8,128)(2,1)S(1)}, bf16[2,272,512]{2,1,0:T(8,128)(2,1)}) fusion(bf16[2,4,272,512]{3,2,1,0:T(8,128)(2,1)} %collective-permute-done, bf16[2,4,272,512]{3,2,1,0:T(8,128)(2,1)} %get-tuple-element.140), kind=kLoop, calls=%fused_computation.7 | loop fusion | flops 4456448 | bytes 6684672 | tf_op jit(solution)/shard_map/convert_element_type | solution.py:1033
  103.1 1.7 collective-permute-start.2
  106.3 45.4 %shard_map.377 = (bf16[4,272,512]{2,1,0:T(8,128)(2,1)}, bf16[4,272,512]{2,1,0:T(8,128)(2,1)}, bf16[2048,1536]{1,0:T(8,128)(2,1)}) custom-call(s32[3]{0:T(128)} %pad_add_fusion.side_ref, f32[8,512]{1,0:T(8,128)} %get-tuple-element.133.small_mlp_ref, f32[8,512]{1,0:T(8,128)} %get-tuple-element.136.small_branch_ref, f32[56,512]{1,0:T(8,128)} %get-tuple-element.137.crpe_ref, ...), custom_call_target="tpu_custom_call" | custom-call | flops 49999998976 | bytes 50000000 | tf_op jit(solution)/shard_map/pallas_call | solution.py:1059
  151.9 1.7 fusion.5
  155.2 1.5 collective-permute-start.5
  160.2 7.9 %shard_map.378 = (f32[4,1024,128]{2,1,0:T(8,128)}, f32[8,512]{1,0:T(8,128)}) custom-call(bf16[512,1536]{1,0:T(8,128)(2,1)} %qkv_ref.5, bf16[512]{0:T(512)(128)(2,1)} %gain_ref.7, bf16[2048,1536]{1,0:T(8,128)(2,1)} %get-tuple-element.175.projected_in, f32[4,2048,128]{2,1,0:T(8,128)} %get-tuple-element.163.parts_in, ...), custom_call_target="tpu_custom_call" | custom-call | flops 8000000000 | bytes 8000000 | tf_op jit(solution)/shard_map/pallas_call | solution.py:1059
  169.2 3.2 %collective-permute-done.8 = bf16[272,512]{1,0:T(8,128)(2,1)} collective-permute-done((bf16[272,512]{1,0:T(8,128)(2,1)S(1)}, bf16[272,512]{1,0:T(8,128)(2,1)}, u32[]{:S(2)}, u32[]{:S(2)}) %collective-permute-start.8) | collective-permute-done | bytes 278560 | tf_op jit(solution)/shard_map/ppermute | solution.py:1039
  173.6 2.4 collective-permute-start.9
  176.5 11.2 %shard_map.379.small_taps_ref = f32[56,512]{1,0:T(8,128)} custom-call(f32[4,2304,128]{2,1,0:T(8,128)} %get-tuple-element.172.back_in, f32[4,2304,128]{2,1,0:T(8,128)} %get-tuple-element.143.query_in, f32[4,2304,128]{2,1,0:T(8,128)} %get-tuple-element.145.value_in), custom_call_target="tpu_custom_call" | custom-call | flops 15000000512 | bytes 15000000 | tf_op jit(solution)/shard_map/pallas_call | solution.py:1059
  188.9 1.5 collective-permute-start.12
  192.4 12.1 %shard_map.380 = (f32[4,1024,128]{2,1,0:T(8,128)}, bf16[80,512]{1,0:T(8,128)(2,1)}) custom-call(bf16[512,1536]{1,0:T(8,128)(2,1)} %qkv_ref.5, bf16[512]{0:T(512)(128)(2,1)} %gain_ref.7, bf16[2048,1536]{1,0:T(8,128)(2,1)} %get-tuple-element.175.projected_in, f32[4,2048,128]{2,1,0:T(8,128)} %get-tuple-element.163.parts_in, ...), custom_call_target="tpu_custom_call" | custom-call | flops 12000000000 | bytes 12000000 | tf_op jit(solution)/shard_map/pallas_call | solution.py:1059
  207.5 1.5 collective-permute-start.17
  209.0 4.2 %shard_map.381 = bf16[1968,512]{1,0:T(8,128)(2,1)} custom-call(bf16[2048,512]{1,0:T(8,128)(2,1)} %get-tuple-element.185.result_ref, f32[2048,128]{1,0:T(8,128)} %get-tuple-element.131.mask_ref.mask_in), custom_call_target="tpu_custom_call" | custom-call | flops 1000000 | bytes 1000 | tf_op jit(solution)/shard_map/pallas_call | solution.py:1059
  214.6 7.9 %shard_map.382 = bf16[1968,512]{1,0:T(8,128)(2,1)} custom-call(f32[2048,128]{1,0:T(8,128)} %get-tuple-element.131.mask_ref.mask_in, bf16[9,512]{1,0:T(8,128)(2,1)} %cpe_ref.3, f32[4,1024,128]{2,1,0:T(8,128)} %get-tuple-element.176.grad_first_in.first_in, f32[4,1024,128]{2,1,0:T(8,128)} %get-tuple-element.192.second_in), custom_call_target="tpu_custom_call" | custom-call | flops 1000000 | bytes 1000 | tf_op jit(solution)/shard_map/pallas_call | solution.py:1059
  226.0 2.9 %shard_map.383 = (f32[512,512]{1,0:T(8,128)}, f32[512,512]{1,0:T(8,128)}, f32[512]{0:T(512)}) custom-call(s32[3]{0:T(128)} %pad_add_fusion.side_ref, bf16[272,512]{1,0:T(8,128)(2,1)} %copy-done.2, bf16[272,512]{1,0:T(8,128)(2,1)} %copy-done.9, bf16[272,512]{1,0:T(8,128)(2,1)} %copy-done.8, bf16[272,512]{1,0:T(8,128)(2,1)} %copy-done.10), custom_call_target="tpu_custom_call" | custom-call | flops 1000000 | bytes 1000 | tf_op jit(solution)/shard_map/pallas_call | solution.py:1059
  229.1 2.5 %collective-permute-start.27 = (bf16[80,512]{1,0:T(8,128)(2,1)S(1)}, bf16[80,512]{1,0:T(8,128)(2,1)S(1)}, u32[]{:S(2)}, u32[]{:S(2)}) collective-permute-start(bf16[80,512]{1,0:T(8,128)(2,1)S(1)} %add_convert_fusion.16), channel_id=1, source_target_pairs={{0,24},{1,25},{2,26},{3,27},{4,28},{5,29},{6,30},{7,31},{8,16},{9,... | collective-permute-start | bytes 245768 | tf_op jit(solution)/shard_map/ppermute | solution.py:1039
  231.7 1.9 collective-permute-start.25
  233.6 4.4 %shard_map.384 = (f32[512,1536]{1,0:T(8,128)}, f32[512,512]{1,0:T(8,128)}, f32[512]{0:T(512)}, f32[512]{0:T(512)}, f32[512]{0:T(512)}, /*index=5*/f32[512]{0:T(512)}, f32[512]{0:T(512)}, f32[512]{0:T(512)}, f32[512]{0:T(512)}) custom-call(s32[3]{0:T(128)} %pad_add_fusion.side_ref, bf16[272,512]{1,0:T(8,128)(2,1)} %copy-done, bf16[272,512]{1,0:T(8,128)(2,1)} %copy-done.5, ...), custom_call_target="tpu_custom_call" | custom-call | flops 1000000 | bytes 1000 | tf_op jit(solution)/shard_map/pallas_call | solution.py:1059
  239.4 1.8 shard_map.385
  (85 shorter events, 23.1 us)
Async XLA Ops:
  7.2 40.6 %all-gather.3.cloned.1.call-start = ((), (), s32[]{:S(2)}) async-start(), calls=%async_computation | async-start | bytes 5324800 | tf_op jit(solution)/shard_map/all_gather | solution.py:1093
  92.3 6.8 %collective-permute-start = (bf16[2,4,272,512]{3,2,1,0:T(8,128)(2,1)}, bf16[2,4,272,512]{3,2,1,0:T(8,128)(2,1)}, u32[]{:S(2)}, u32[]{:S(2)}) collective-permute-start(bf16[2,4,272,512]{3,2,1,0:T(8,128)(2,1)} %get-tuple-element.141), channel_id=1, source_target_pairs={{0,1},{1,0},{2,3},{3,2},{4,5},{5,4},{6,7},{7,6},{8,9},{9,8},{10,11... | collective-permute-start | bytes 6684680 | tf_op jit(solution)/shard_map/ppermute | solution.py:1039
  102.8 48.9 %collective-permute-start.1 = (bf16[2,272,512]{2,1,0:T(8,128)(2,1)}, bf16[2,272,512]{2,1,0:T(8,128)(2,1)}, u32[]{:S(2)}, u32[]{:S(2)}) collective-permute-start(bf16[2,272,512]{2,1,0:T(8,128)(2,1)} %get-tuple-element.152), channel_id=1, source_target_pairs={{0,2},{1,3},{2,0},{3,1},{4,6},{5,7},{6,4},{7,5},{8,10},{9,11},{10,... | collective-permute-start | bytes 1671176 | tf_op jit(solution)/shard_map/ppermute | solution.py:1039
  103.1 48.7 %collective-permute-start.2 = (bf16[2,272,512]{2,1,0:T(8,128)(2,1)S(1)}, bf16[2,272,512]{2,1,0:T(8,128)(2,1)}, u32[]{:S(2)}, u32[]{:S(2)}) collective-permute-start(bf16[2,272,512]{2,1,0:T(8,128)(2,1)S(1)} %get-tuple-element.153), channel_id=1, source_target_pairs={{0,4},{1,5},{2,6},{3,7},{4,0},{5,1},{6,2},{7,3},{8,12},{9,13},{10,... | collective-permute-start | bytes 1671176 | tf_op jit(solution)/shard_map/ppermute | solution.py:1039
  104.8 47.0 %collective-permute-start.3 = (bf16[2,272,512]{2,1,0:T(8,128)(2,1)S(1)}, bf16[2,272,512]{2,1,0:T(8,128)(2,1)}, u32[]{:S(2)}, u32[]{:S(2)}) collective-permute-start(bf16[2,272,512]{2,1,0:T(8,128)(2,1)S(1)} %get-tuple-element.154), channel_id=1, source_target_pairs={{0,6},{1,7},{2,4},{3,5},{4,2},{5,3},{6,0},{7,1},{8,14},{9,15},{10,... | collective-permute-start | bytes 1671176 | tf_op jit(solution)/shard_map/ppermute | solution.py:1039
  155.2 13.0 %collective-permute-start.5 = (bf16[272,512]{1,0:T(8,128)(2,1)S(1)}, bf16[272,512]{1,0:T(8,128)(2,1)}, u32[]{:S(2)}, u32[]{:S(2)}) collective-permute-start(bf16[272,512]{1,0:T(8,128)(2,1)S(1)} %get-tuple-element.167), channel_id=1, source_target_pairs={{0,8},{1,9},{2,10},{3,11},{4,12},{5,13},{6,14},{7,15},{8,0},{9,1},... | collective-permute-start | bytes 835592 | tf_op jit(solution)/shard_map/ppermute | solution.py:1039
  156.7 12.5 %collective-permute-start.6 = (bf16[272,512]{1,0:T(8,128)(2,1)S(1)}, bf16[272,512]{1,0:T(8,128)(2,1)S(1)}, u32[]{:S(2)}, u32[]{:S(2)}) collective-permute-start(bf16[272,512]{1,0:T(8,128)(2,1)S(1)} %get-tuple-element.169), channel_id=1, source_target_pairs={{0,2},{1,3},{2,0},{3,1},{4,6},{5,7},{6,4},{7,5},{8,10},{9,11},{10,... | collective-permute-start | bytes 835592 | tf_op jit(solution)/shard_map/ppermute | solution.py:1039
  157.3 11.9 %collective-permute-start.7 = (bf16[272,512]{1,0:T(8,128)(2,1)S(1)}, bf16[272,512]{1,0:T(8,128)(2,1)}, u32[]{:S(2)}, u32[]{:S(2)}) collective-permute-start(bf16[272,512]{1,0:T(8,128)(2,1)S(1)} %get-tuple-element.170), channel_id=1, source_target_pairs={{0,4},{1,5},{2,6},{3,7},{4,0},{5,1},{6,2},{7,3},{8,12},{9,13},{10,... | collective-permute-start | bytes 835592 | tf_op jit(solution)/shard_map/ppermute | solution.py:1039
  158.7 13.7 %collective-permute-start.8 = (bf16[272,512]{1,0:T(8,128)(2,1)S(1)}, bf16[272,512]{1,0:T(8,128)(2,1)}, u32[]{:S(2)}, u32[]{:S(2)}) collective-permute-start(bf16[272,512]{1,0:T(8,128)(2,1)S(1)} %get-tuple-element.171), channel_id=1, source_target_pairs={{0,6},{1,7},{2,4},{3,5},{4,2},{5,3},{6,0},{7,1},{8,14},{9,15},{10,... | collective-permute-start | bytes 835592 | tf_op jit(solution)/shard_map/ppermute | solution.py:1039
  173.6 14.3 %collective-permute-start.9 = (bf16[272,512]{1,0:T(8,128)(2,1)S(1)}, bf16[272,512]{1,0:T(8,128)(2,1)S(1)}, u32[]{:S(2)}, u32[]{:S(2)}) collective-permute-start(bf16[272,512]{1,0:T(8,128)(2,1)S(1)} %add_convert_fusion.8), channel_id=1, source_target_pairs={{0,16},{1,17},{2,18},{3,19},{4,20},{5,21},{6,22},{7,23},{8,24},{9,... | collective-permute-start | bytes 835592 | tf_op jit(solution)/shard_map/ppermute | solution.py:1039
  176.0 12.8 %collective-permute-start.10 = (bf16[272,512]{1,0:T(8,128)(2,1)S(1)}, bf16[272,512]{1,0:T(8,128)(2,1)S(1)}, u32[]{:S(2)}, u32[]{:S(2)}) collective-permute-start(bf16[272,512]{1,0:T(8,128)(2,1)S(1)} %add_convert_fusion.7), channel_id=1, source_target_pairs={{0,8},{1,9},{2,10},{3,11},{4,12},{5,13},{6,14},{7,15},{8,0},{9,1},... | collective-permute-start | bytes 835592 | tf_op jit(solution)/shard_map/ppermute | solution.py:1039
  188.9 15.9 %collective-permute-start.12 = (bf16[272,512]{1,0:T(8,128)(2,1)S(1)}, bf16[272,512]{1,0:T(8,128)(2,1)S(1)}, u32[]{:S(2)}, u32[]{:S(2)}) collective-permute-start(bf16[272,512]{1,0:T(8,128)(2,1)S(1)} %add_convert_fusion.6.first_ref), channel_id=1, source_target_pairs={{0,4},{1,5},{2,6},{3,7},{4,0},{5,1},{6,2},{7,3},{8,12},{9,13},{10,... | collective-permute-start | bytes 835592 | tf_op jit(solution)/shard_map/ppermute | solution.py:1039
  190.4 14.4 %collective-permute-start.11 = (bf16[272,512]{1,0:T(8,128)(2,1)S(1)}, bf16[272,512]{1,0:T(8,128)(2,1)S(1)}, u32[]{:S(2)}, u32[]{:S(2)}) collective-permute-start(bf16[272,512]{1,0:T(8,128)(2,1)S(1)} %add_convert_fusion.6.first_ref), channel_id=1, source_target_pairs={{0,8},{1,9},{2,10},{3,11},{4,12},{5,13},{6,14},{7,15},{8,0},{9,1},... | collective-permute-start | bytes 835592 | tf_op jit(solution)/shard_map/ppermute | solution.py:1039
  190.9 13.8 %collective-permute-start.13 = (bf16[272,512]{1,0:T(8,128)(2,1)S(1)}, bf16[272,512]{1,0:T(8,128)(2,1)S(1)}, u32[]{:S(2)}, u32[]{:S(2)}) collective-permute-start(bf16[272,512]{1,0:T(8,128)(2,1)S(1)} %add_convert_fusion.5), channel_id=1, source_target_pairs={{0,16},{1,17},{2,18},{3,19},{4,20},{5,21},{6,22},{7,23},{8,24},{9,... | collective-permute-start | bytes 835592 | tf_op jit(solution)/shard_map/ppermute | solution.py:1039
  204.8 9.6 %collective-permute-start.15 = (bf16[272,512]{1,0:T(8,128)(2,1)S(1)}, bf16[272,512]{1,0:T(8,128)(2,1)S(1)}, u32[]{:S(2)}, u32[]{:S(2)}) collective-permute-start(bf16[272,512]{1,0:T(8,128)(2,1)S(1)} %collective-permute-done.11.second_ref), channel_id=1, source_target_pairs={{0,4},{1,5},{2,6},{3,7},{4,0},{5,1},{6,2},{7,3},{8,12},{9,13},{10,... | collective-permute-start | bytes 835592 | tf_op jit(solution)/shard_map/ppermute | solution.py:1039
  205.4 7.7 %collective-permute-start.14 = (bf16[80,512]{1,0:T(8,128)(2,1)}, bf16[80,512]{1,0:T(8,128)(2,1)S(1)}, u32[]{:S(2)}, u32[]{:S(2)}) collective-permute-start(bf16[80,512]{1,0:T(8,128)(2,1)} %get-tuple-element.189), channel_id=1, source_target_pairs={{0,1},{1,0},{2,3},{3,2},{4,5},{5,4},{6,7},{7,6},{8,9},{9,8},{10,11... | collective-permute-start | bytes 245768 | tf_op jit(solution)/shard_map/ppermute | solution.py:1039
  205.5 16.9 %collective-permute-start.19 = (bf16[272,512]{1,0:T(8,128)(2,1)S(1)}, bf16[272,512]{1,0:T(8,128)(2,1)S(1)}, u32[]{:S(2)}, u32[]{:S(2)}) collective-permute-start(bf16[272,512]{1,0:T(8,128)(2,1)S(1)} %add_convert_fusion.4.refs_0_), channel_id=1, source_target_pairs={{0,6},{1,7},{2,4},{3,5},{4,2},{5,3},{6,0},{7,1},{8,14},{9,15},{10,... | collective-permute-start | bytes 835592 | tf_op jit(solution)/shard_map/ppermute | solution.py:1039
  206.9 16.6 %collective-permute-start.18 = (bf16[272,512]{1,0:T(8,128)(2,1)S(1)}, bf16[272,512]{1,0:T(8,128)(2,1)S(1)}, u32[]{:S(2)}, u32[]{:S(2)}) collective-permute-start(bf16[272,512]{1,0:T(8,128)(2,1)S(1)} %add_convert_fusion.4.refs_0_), channel_id=1, source_target_pairs={{0,4},{1,5},{2,6},{3,7},{4,0},{5,1},{6,2},{7,3},{8,12},{9,13},{10,... | collective-permute-start | bytes 835592 | tf_op jit(solution)/shard_map/ppermute | solution.py:1039
  207.5 15.9 %collective-permute-start.17 = (bf16[272,512]{1,0:T(8,128)(2,1)S(1)}, bf16[272,512]{1,0:T(8,128)(2,1)S(1)}, u32[]{:S(2)}, u32[]{:S(2)}) collective-permute-start(bf16[272,512]{1,0:T(8,128)(2,1)S(1)} %add_convert_fusion.4.refs_0_), channel_id=1, source_target_pairs={{0,2},{1,3},{2,0},{3,1},{4,6},{5,7},{6,4},{7,5},{8,10},{9,11},{10,... | collective-permute-start | bytes 835592 | tf_op jit(solution)/shard_map/ppermute | solution.py:1039
  214.5 8.9 %collective-permute-start.16 = (bf16[80,512]{1,0:T(8,128)(2,1)S(1)}, bf16[80,512]{1,0:T(8,128)(2,1)S(1)}, u32[]{:S(2)}, u32[]{:S(2)}) collective-permute-start(bf16[80,512]{1,0:T(8,128)(2,1)S(1)} %add_convert_fusion.18), channel_id=1, source_target_pairs={{0,2},{1,3},{2,0},{3,1},{4,6},{5,7},{6,4},{7,5},{8,10},{9,11},{10,... | collective-permute-start | bytes 245768 | tf_op jit(solution)/shard_map/ppermute | solution.py:1039
  223.5 5.6 %collective-permute-start.21 = (bf16[272,512]{1,0:T(8,128)(2,1)S(1)}, bf16[272,512]{1,0:T(8,128)(2,1)S(1)}, u32[]{:S(2)}, u32[]{:S(2)}) collective-permute-start(bf16[272,512]{1,0:T(8,128)(2,1)S(1)} %add_convert_fusion.4.refs_0_), channel_id=1, source_target_pairs={{0,1},{1,0},{2,3},{3,2},{4,5},{5,4},{6,7},{7,6},{8,9},{9,8},{10,11... | collective-permute-start | bytes 835592 | tf_op jit(solution)/shard_map/ppermute | solution.py:1039
  229.1 8.9 %collective-permute-start.27 = (bf16[80,512]{1,0:T(8,128)(2,1)S(1)}, bf16[80,512]{1,0:T(8,128)(2,1)S(1)}, u32[]{:S(2)}, u32[]{:S(2)}) collective-permute-start(bf16[80,512]{1,0:T(8,128)(2,1)S(1)} %add_convert_fusion.16), channel_id=1, source_target_pairs={{0,24},{1,25},{2,26},{3,27},{4,28},{5,29},{6,30},{7,31},{8,16},{9,... | collective-permute-start | bytes 245768 | tf_op jit(solution)/shard_map/ppermute | solution.py:1039
  231.7 7.1 %collective-permute-start.26 = (bf16[80,512]{1,0:T(8,128)(2,1)S(1)}, bf16[80,512]{1,0:T(8,128)(2,1)S(1)}, u32[]{:S(2)}, u32[]{:S(2)}) collective-permute-start(bf16[80,512]{1,0:T(8,128)(2,1)S(1)} %add_convert_fusion.16), channel_id=1, source_target_pairs={{0,16},{1,17},{2,18},{3,19},{4,20},{5,21},{6,22},{7,23},{8,24},{9,... | collective-permute-start | bytes 245768 | tf_op jit(solution)/shard_map/ppermute | solution.py:1039
  231.7 7.1 %collective-permute-start.25 = (bf16[80,512]{1,0:T(8,128)(2,1)S(1)}, bf16[80,512]{1,0:T(8,128)(2,1)S(1)}, u32[]{:S(2)}, u32[]{:S(2)}) collective-permute-start(bf16[80,512]{1,0:T(8,128)(2,1)S(1)} %add_convert_fusion.16), channel_id=1, source_target_pairs={{0,8},{1,9},{2,10},{3,11},{4,12},{5,13},{6,14},{7,15},{8,0},{9,1},... | collective-permute-start | bytes 245768 | tf_op jit(solution)/shard_map/ppermute | solution.py:1039
  (17 other events, 128.8 us)
Sparse Core Ops, SparseCore 0:
  10.2 37.5 all-gather.2
where the time goes:
time: 251 us; the launch traced here: 248 us
  Pallas kernels  184 us (73%)
  starting transfers between devices  26.6 us (11%)
  between operations  15.3 us (6%)
  waiting for transfers between devices  12.5 us (5%)
  other arithmetic  9.55 us (4%)
    pallas_call x13, Pallas kernels, call(): pl.pallas_call(body, out_shape=plain(outs), in_specs=[place(value) for va...  184 us
    ppermute x28, starting transfers between devices, exchange(): lax.ppermute(values, ('dp', 'blk'), [(at, at ^ flip) for at in range(part...  26.5 us
    ppermute x28, waiting for transfers between devices, exchange(): lax.ppermute(values, ('dp', 'blk'), [(at, at ^ flip) for at in range(part...  8.73 us
    convert_element_type x10, other arithmetic, add(): return sum((term.astype(F32) for term in terms)).astype(BF16)  6.56 us
  transfers between devices with their start and end apart: 29, of which 10 were waited for; matrix products, arithmetic and copies ran while one was open for 1% of the time, Pallas kernels for 55%

commit v1 on v0

--- a/solution.py
+++ b/solution.py
@@ -17,7 +17,7 @@
 SLOT_PAD = 96
 TILE = 256
 BAND = 128
-MLP_TILE = 1024
+MLP_TILE = 512
 KERNEL_SIZES = (3, 5, 7, 7)
 PIECE = 256
 VMEM_BYTES = 62 * 1024 * 1024
@@ -492,26 +492,15 @@
 
 def gelu_parts(value):
     level = 0.5 + 0.5 * lax.erf(value * math.sqrt(0.5))
-    return level, jnp.exp2(value * value * (-0.5 / math.log(2.0))) * (1.0 / math.sqrt(2.0 * math.pi))
-
-
-def mlp_kernel(
-    side_ref, cot_ref, mask_ref, second_in, fc_in, gain_ref, shift_ref, fc2_bias_ref,
-    result_out, grad_out, grad_fc_keep, grad_fc_send, small_ref,
-    second_ref, fc_ref, grad_ref, grad_fc_ref,
-    work_ref, cot_rows_ref, cot_t_ref, normed_ref, normed_t_ref, hidden_ref, pre_ref, hidden_two_ref, pre_two_ref, mlp_ref, back_ref,
-    table_ref, result_ref, inverse_ref, sems,
-):
-    fill_table((gain_ref, shift_ref, fc2_bias_ref), table_ref)
+    return level, jnp.exp2(value * value * (-0.5 / math.log(2.0)) - 0.5 * math.log2(2.0 * math.pi))
+
+
+def cotangent_kernel(cot_ref, mask_ref, cot_rows_out, cot_t_out, sums_ref, cot_rows_ref, cot_t_ref, work_ref, sems):
     copies = Copies(sems)
-    got_second = copies.start(second_in, second_ref)
-    got_fc = copies.start(fc_in, fc_ref)
     rows, channels = cot_ref.shape
     blocks = channels // LANES
     images = rows // SLOT
-    padded = normed_ref.shape[0]
-    owners, _, units = fc_ref.shape
-    mine, half_x, half_z = side_ref[1], side_ref[2] & 1, (side_ref[2] >> 1) & 1
+    padded = cot_rows_ref.shape[0]
     spread(cot_ref, work_ref, blocks)
     cot_rows_ref[rows:padded, :] = jnp.zeros((padded - rows, channels), BF16)
 
@@ -529,8 +518,29 @@
         return [sums[block] + fold_rows(parts[block]) for block in range(blocks)]
 
     zero = [jnp.zeros((8, LANES), F32) for _ in range(blocks)]
-    bias_sums = lax.fori_loop(0, SLOT // 2, arrange, zero)
+    sums_ref[...] = jnp.concatenate(lax.fori_loop(0, SLOT // 2, arrange, zero), 1)
+    copies.start(cot_rows_ref, cot_rows_out)
     transpose_rows(cot_rows_ref, cot_t_ref)
+    copies.start(cot_t_ref, cot_t_out)
+    copies.finish()
+
+
+def mlp_kernel(
+    side_ref, bias_sums_ref, cot_rows_in, cot_t_in, second_in, fc_in, gain_ref, shift_ref, fc2_bias_ref,
+    result_out, grad_out, grad_fc_keep, grad_fc_send, small_ref,
+    second_ref, fc_ref, grad_ref, grad_fc_ref,
+    cot_rows_ref, cot_t_ref, normed_ref, normed_t_ref, hidden_ref, pre_ref, hidden_two_ref, pre_two_ref, mlp_ref, back_ref,
+    table_ref, result_ref, inverse_ref, sems,
+):
+    fill_table((gain_ref, shift_ref, fc2_bias_ref), table_ref)
+    copies = Copies(sems)
+    got_second = copies.start(second_in, second_ref)
+    got_fc = copies.start(fc_in, fc_ref)
+    got_cot = [copies.start(cot_rows_in, cot_rows_ref), copies.start(cot_t_in, cot_t_ref)]
+    padded, channels = cot_rows_ref.shape
+    blocks = channels // LANES
+    owners, _, units = fc_ref.shape
+    mine, half_x, half_z = side_ref[1], side_ref[2] & 1, (side_ref[2] >> 1) & 1
     got_second.wait()
     fc2_bias = table_ref[FC2_B : FC2_B + 1, :]
 
@@ -542,68 +552,46 @@
         second_ref, table_ref, GAIN2, SHIFT2, normed_ref, normed_t_ref, second_ref, inverse_ref, keep
     )
     normed_t_ref[channels:, :] = jnp.ones_like(normed_t_ref[channels:, :])
-    half = units // 2
     got_fc.wait()
-
-    full = padded // MLP_TILE
-    wide = units // full
-    ends = 2
-    rows_half = MLP_TILE // ends
-
-    def weights(slot, held, step):
-        cols = pl.ds(pl.multiple_of(step * wide, wide), wide)
-        hidden_ref, pre_ref = held
-        for which, (left_ref, right_ref) in enumerate(((normed_t_ref, pre_ref), (cot_t_ref, hidden_ref))):
-            grad = dot(left_ref[...], right_ref[:, cols]).astype(BF16)
-            for end in range(2):
-                place = ((half_x ^ which) << 1) | (half_z ^ end)
-                grad_fc_ref[slot, place, 0:PIECE, cols] = grad[end * PIECE : (end + 1) * PIECE]
-            if which == 0:
-                grad_fc_ref[slot, (half_x << 1) | half_z, PIECE:, cols] = grad[channels:]
-            yield
+    for copy in got_cot:
+        copy.wait()
+
+    tiles = padded // MLP_TILE
+
+    def weights(slot, held, which, end):
+        left_ref, right_ref = (normed_t_ref, held[1]) if which == 0 else (cot_t_ref, held[0])
+        last = left_ref.shape[0] if end else PIECE
+        grad = dot(left_ref[end * PIECE : last, :], right_ref[...]).astype(BF16)
+        place = ((half_x ^ which) << 1) | (half_z ^ end)
+        grad_fc_ref[slot, place, 0:PIECE, :] = grad[0:PIECE]
+        if last > channels:
+            grad_fc_ref[slot, (half_x << 1) | half_z, PIECE:, :] = grad[PIECE:]
 
     def part(slot, held, before):
         owner = mine ^ ((slot >> 1) | ((slot & 1) << 1))
         hidden_ref, pre_ref = held
-
-        def tile(step):
-            beside = iter(()) if before is None else weights(slot - 1, before, step)
-            for end in range(ends):
-                at = rows_at(step * MLP_TILE + end * rows_half, rows_half, rows_half)
-                normed = normed_ref[at, :]
-                cot = cot_rows_ref[at, :]
-                mlp, back = None, None
-                for piece in range(2):
-                    cols = slice(piece * half, (piece + 1) * half)
-                    first = fc_ref[owner, 0:channels, cols]
-                    second = fc_ref[owner, channels + piece * half : channels + (piece + 1) * half, :]
-                    bias = fc_ref[owner, 2 * channels :, cols].astype(F32)[0:1]
-                    values, grads = dot(normed, first), dot_nt(cot, second)
-                    if piece == 0:
-                        next(beside, None)
-                    values = values + bias
-                    level, density = gelu_parts(values)
-                    hidden = (values * level).astype(BF16)
-                    pre = (grads * (level + values * density)).astype(BF16)
-                    hidden_ref[at, cols] = hidden
-                    pre_ref[at, cols] = pre
-                    more_mlp, more_back = dot(hidden, second), dot_nt(pre, first)
-                    mlp = more_mlp if mlp is None else mlp + more_mlp
-                    back = more_back if back is None else back + more_back
-                if slot == 0:
-                    back_ref[at, :] = back
-                else:
-                    back_ref[at, :] += back
-                if slot < owners - 1:
-                    mlp_ref[at, :] += mlp
-                else:
-                    result_ref[at, :] = (mlp_ref[at, :] + mlp).astype(BF16)
-
-        loop(full, tile)
-
-    def last_weights(step):
-        for _ in weights(owners - 1, held[(owners - 1) % 2], step):
-            pass
+        for step in range(tiles):
+            at = slice(step * MLP_TILE, (step + 1) * MLP_TILE)
+            first = fc_ref[owner, 0:channels, :]
+            second = fc_ref[owner, channels : 2 * channels, :]
+            bias = fc_ref[owner, 2 * channels :, :].astype(F32)[0:1]
+            values, grads = dot(normed_ref[at, :], first) + bias, dot_nt(cot_rows_ref[at, :], second)
+            if before is not None and step < 4:
+                weights(slot - 1, before, step // 2, step % 2)
+            level, density = gelu_parts(values)
+            hidden = (values * level).astype(BF16)
+            pre = (grads * (level + values * density)).astype(BF16)
+            hidden_ref[at, :] = hidden
+            pre_ref[at, :] = pre
+            mlp, back = dot(hidden, second), dot_nt(pre, first)
+            if slot == 0:
+                back_ref[at, :] = back
+            else:
+                back_ref[at, :] += back
+            if slot < owners - 1:
+                mlp_ref[at, :] += mlp
+            else:
+                result_ref[at, :] = (mlp_ref[at, :] + mlp).astype(BF16)
 
     held = (hidden_ref, pre_ref), (hidden_two_ref, pre_two_ref)
     targets = [(grad_fc_keep if slot < owners // 2 else grad_fc_send).at[slot % (owners // 2)] for slot in range(owners)]
@@ -611,7 +599,8 @@
         if slot < owners:
             part(slot, held[slot % 2], held[(slot - 1) % 2] if slot else None)
         else:
-            loop(full, last_weights)
+            for step in range(4):
+                weights(owners - 1, held[(owners - 1) % 2], step // 2, step % 2)
         if slot:
             copies.start(grad_fc_ref.at[slot - 1], targets[slot - 1])
 
@@ -633,8 +622,8 @@
     small_ref[...] = jnp.zeros_like(small_ref)
     small_ref[0:1, :] = total_row(gain_sums)
     small_ref[1:2, :] = total_row(shift_sums)
-    small_ref[2:3, :] = total_row(bias_sums)
-    for copy in copies.open[2:]:
+    small_ref[2:3, :] = jnp.sum(bias_sums_ref[...], 0, keepdims=True)
+    for copy in copies.open[4:]:
         copy.wait()
 
 
@@ -985,11 +974,12 @@
 
 
 def finish_small_kernel(
-    small_ref,
+    own_ref, first_ref, second_ref, third_ref,
     cpe_ref, cpe_bias_ref, gain_ref, shift_ref, crpe_small_ref, crpe_middle_ref, crpe_large_ref,
     work_ref,
 ):
-    small = small_ref[...]
+    terms = [ref[...].astype(F32) for ref in (own_ref, first_ref, second_ref, third_ref)]
+    small = ((terms[0] + terms[1]) + (terms[2] + terms[3])).astype(BF16)
     work_ref[...] = small.astype(F32)
     cpe_ref[...] = work_ref[64:73, :]
     for row, ref in enumerate((cpe_bias_ref, gain_ref, shift_ref)):
@@ -1112,6 +1102,14 @@
         cpe_bias, norm1_gain, norm1_shift, query_bias, value_bias, crpe_bias, proj_bias,
     )
     pieces = (owners // 2, 4, PIECE + 16, units)
+    cot_shapes = [((padded, channels), BF16), ((channels, padded), BF16)]
+    cot_rows, cot_t, cot_sums = call(
+        cotangent_kernel,
+        [Held(shape(*item)) for item in cot_shapes] + [shape((8, channels), F32)],
+        cot_shapes + [((blocks, rows, LANES), F32), 2],
+        6_000_000_000,
+        cotangent, mask,
+    )
     result, grad_second, fc_keep, fc_send, small_mlp = call(
         mlp_kernel,
         [
@@ -1122,14 +1120,13 @@
         [
             (block_rows, F32), (fc_all.shape, BF16), (block_rows, F32),
             ((owners, 4, PIECE + 16, units), BF16),
-            ((blocks, rows, LANES), F32),
             ((padded, channels), BF16), ((channels, padded), BF16),
             ((padded, channels), BF16), ((channels + 16, padded), BF16),
             ((padded, units), BF16), ((padded, units), BF16), ((padded, units), BF16), ((padded, units), BF16),
-            ((padded, channels), F32), ((padded, channels), F32), ((8, channels), F32), ((padded, channels), BF16), ((padded, LANES), F32), 4 + owners,
+            ((padded, channels), F32), ((padded, channels), F32), ((8, channels), F32), ((padded, channels), BF16), ((padded, LANES), F32), 6 + owners,
         ],
         60_000_000_000,
-        scalars, cotangent, mask, Held(second), Held(fc_all), norm2_gain, norm2_shift, fc2_bias,
+        scalars, cot_sums, Held(cot_rows), Held(cot_t), Held(second), Held(fc_all), norm2_gain, norm2_shift, fc2_bias,
     )
     fc_far = exchange(fc_send, 0, 1)
     back, grad_proj, small_branch = call(
@@ -1246,6 +1243,8 @@
     )
     fc1, small, small_far, *total_pieces = together(fc1, small, small_far, *total_pieces)
     small = add(small, small_far)
+    for bit in bits[2:]:
+        small = add(small, exchange(small, bit, 0))
     small_far = [exchange(small, flip, 0) for flip in (bits[0], bits[1], bits[0] | bits[1])]
     row = shape((channels,), F32)
     grad_qkv, grad_proj, query_sums, value_sums, crpe_sums, proj_sums, gain_two, shift_two, fc2_sums = call(
@@ -1259,10 +1258,6 @@
         scalars, *total_pieces,
     )
     grad_qkv, small, *small_far = together(grad_qkv, small, *small_far)
-    terms = [term.astype(F32) for term in (small, *small_far)]
-    small = ((terms[0] + terms[1]) + (terms[2] + terms[3])).astype(BF16)
-    for bit in bits[2:]:
-        small = add(small, exchange(small, bit, 0))
     cpe, cpe_sums, gain_one, shift_one, taps_small, taps_middle, taps_large = call(
         finish_small_kernel,
         [
@@ -1271,7 +1266,7 @@
         ],
         [((80, channels), F32)],
         1_000_000,
-        small,
+        small, *small_far,
     )
     return (
         output, grad_tokens, cpe, cpe_sums, gain_one, shift_one, grad_qkv, query_sums, value_sums,

time: 251 us -> 243 us (0.968)
  Pallas kernels: 184 us -> 177 us
  waiting for transfers between devices: 12.5 us -> 6.52 us
  starting transfers between devices: 26.6 us -> 30.2 us
    pallas_call x13 -> x14, Pallas kernels: 184 us -> 177 us  [call(): pl.pallas_call(body, out_shape=plain(outs), in_specs=[place(value) for va...]
    all_gather x1, waiting for transfers between devices: 3.77 us -> 0.02 us  [shards(): fc_all = lax.all_gather(packed, 'blk', axis=0, tiled=False)]
    ppermute x28, starting transfers between devices: 26.5 us -> 30.2 us  [exchange(): lax.ppermute(values, ('dp', 'blk'), [(at, at ^ flip) for at in range(part...]
  transfers between devices with their start and end apart: 29 -> 29, of which waited for: 10 -> 6; matrix products, arithmetic and copies ran while one was open for 1% -> 1% of each run, Pallas kernels for 55% -> 55%
where the time goes in v1:
time: 243 us; the launch traced here: 239 us
  Pallas kernels  177 us (73%)
  starting transfers between devices  30.2 us (12%)
  between operations  15.3 us (6%)
  other arithmetic  8.88 us (4%)
  waiting for transfers between devices  6.52 us (3%)
    pallas_call x14, Pallas kernels, call(): pl.pallas_call(body, out_shape=plain(outs), in_specs=[place(value) for va...  177 us
    ppermute x28, starting transfers between devices, exchange(): lax.ppermute(values, ('dp', 'blk'), [(at, at ^ flip) for at in range(part...  30.2 us
    convert_element_type x10, other arithmetic, add(): return sum((term.astype(F32) for term in terms)).astype(BF16)  6.56 us
    ppermute x28, waiting for transfers between devices, exchange(): lax.ppermute(values, ('dp', 'blk'), [(at, at ^ flip) for at in range(part...  6.48 us
  transfers between devices with their start and end apart: 29, of which 6 were waited for; matrix products, arithmetic and copies ran while one was open for 1% of the time, Pallas kernels for 55%

profile of v1, /device:TPU:0, one launch (start us, length us, event | category | flops | bytes accessed | tf_op | source)
XLA Modules:
  0.0 238.8 jit_solution(10693028572420776903)
XLA Ops:
  7.2 2.3 shard_map.375
  10.8 33.2 %shard_map.373 = (f32[56,512]{1,0:T(8,128)}, f32[2048,128]{1,0:T(8,128)}, f32[4,2048,128]{2,1,0:T(8,128)}, f32[4,2048,128]{2,1,0:T(8,128)}, f32[2048,128]{1,0:T(...) custom-call(s32[3]{0:T(128)} %pad_add_fusion.side_ref, ...), custom_call_target="tpu_custom_call" | custom-call | flops 40000000000 | bytes 40000000 | tf_op jit(solution)/shard_map/pallas_call | solution.py:1049
  44.0 5.8 %shard_map.374 = (bf16[2048,512]{1,0:T(8,128)(2,1)}, bf16[512,2048]{1,0:T(8,128)(2,1)}, f32[8,512]{1,0:T(8,128)}) custom-call(bf16[1968,512]{1,0:T(8,128)(2,1)} %cot_ref.1, f32[2048,128]{1,0:T(8,128)} %get-tuple-element.134.mask_ref.mask_in), custom_call_target="tpu_custom_call" | custom-call | flops 6000000000 | bytes 6000000 | tf_op jit(solution)/shard_map/pallas_call | solution.py:1049
  49.9 41.3 %shard_map.376 = (bf16[2048,512]{1,0:T(8,128)(2,1)}, f32[4,2048,128]{2,1,0:T(8,128)}, bf16[2,4,272,512]{3,2,1,0:T(8,128)(2,1)}, bf16[2,4,272,512]{3,2,1,0:T(8,128)(2,1)}, f32[8,512]{1,0:T(8,128)}) custom-call(s32[3]{0:T(128)} %pad_add_fusion.side_ref, f32[8,512]{1,0:T(8,128)} %get-tuple-element.135.bias_sums_ref, ...), custom_call_target="tpu_custom_call" | custom-call | flops 60000002048 | bytes 60000000 | tf_op jit(solution)/shard_map/pallas_call | solution.py:1049
  91.7 6.5 %shard_map.377 = (f32[4,2304,128]{2,1,0:T(8,128)}, bf16[512,512]{1,0:T(8,128)(2,1)}, f32[8,512]{1,0:T(8,128)}) custom-call(bf16[512,512]{1,0:T(8,128)(2,1)} %proj_ref.3, f32[4,2048,128]{2,1,0:T(8,128)} %get-tuple-element.140.grad_in, bf16[512,2048]{1,0:T(8,128)(2,1)} %get-tuple-element.141.attended_t_in), custom_call_target="tpu_custom_call" | custom-call | flops 10000000000 | bytes 10000000 | tf_op jit(solution)/shard_map/pallas_call | solution.py:1049
  98.2 3.7 %fusion.3 = (bf16[2,272,512]{2,1,0:T(8,128)(2,1)S(1)}, bf16[2,272,512]{2,1,0:T(8,128)(2,1)S(1)}, bf16[2,272,512]{2,1,0:T(8,128)(2,1)S(1)}, bf16[2,272,512]{2,1,0:T(8,128)(2,1)}) fusion(bf16[2,4,272,512]{3,2,1,0:T(8,128)(2,1)} %collective-permute-done, bf16[2,4,272,512]{3,2,1,0:T(8,128)(2,1)} %get-tuple-element.146), kind=kLoop, calls=%fused_computation.7 | loop fusion | flops 4456448 | bytes 6684672 | tf_op jit(solution)/shard_map/convert_element_type | solution.py:1023
  102.0 2.5 %collective-permute-start.1 = (bf16[2,272,512]{2,1,0:T(8,128)(2,1)}, bf16[2,272,512]{2,1,0:T(8,128)(2,1)}, u32[]{:S(2)}, u32[]{:S(2)}) collective-permute-start(bf16[2,272,512]{2,1,0:T(8,128)(2,1)} %get-tuple-element.158), channel_id=1, source_target_pairs={{0,2},{1,3},{2,0},{3,1},{4,6},{5,7},{6,4},{7,5},{8,10},{9,11},{10,... | collective-permute-start | bytes 1671176 | tf_op jit(solution)/shard_map/ppermute | solution.py:1029
  106.0 35.2 %shard_map.378 = (bf16[4,272,512]{2,1,0:T(8,128)(2,1)}, bf16[4,272,512]{2,1,0:T(8,128)(2,1)}, bf16[2048,1536]{1,0:T(8,128)(2,1)}) custom-call(s32[3]{0:T(128)} %pad_add_fusion.side_ref, f32[8,512]{1,0:T(8,128)} %get-tuple-element.139.small_mlp_ref, f32[8,512]{1,0:T(8,128)} %get-tuple-element.142.small_branch_ref, f32[56,512]{1,0:T(8,128)} %get-tuple-element.143.crpe_ref, ...), custom_call_target="tpu_custom_call" | custom-call | flops 49999998976 | bytes 50000000 | tf_op jit(solution)/shard_map/pallas_call | solution.py:1049
  141.4 1.7 fusion.5
  144.7 2.1 collective-permute-start.5
  150.2 7.9 %shard_map.379 = (f32[4,1024,128]{2,1,0:T(8,128)}, f32[8,512]{1,0:T(8,128)}) custom-call(bf16[512,1536]{1,0:T(8,128)(2,1)} %qkv_ref.5, bf16[512]{0:T(512)(128)(2,1)} %gain_ref.7, bf16[2048,1536]{1,0:T(8,128)(2,1)} %get-tuple-element.181.projected_in, f32[4,2048,128]{2,1,0:T(8,128)} %get-tuple-element.169.parts_in, ...), custom_call_target="tpu_custom_call" | custom-call | flops 8000000000 | bytes 8000000 | tf_op jit(solution)/shard_map/pallas_call | solution.py:1049
  159.2 3.2 %collective-permute-done.8 = bf16[272,512]{1,0:T(8,128)(2,1)} collective-permute-done((bf16[272,512]{1,0:T(8,128)(2,1)S(1)}, bf16[272,512]{1,0:T(8,128)(2,1)}, u32[]{:S(2)}, u32[]{:S(2)}) %collective-permute-start.8) | collective-permute-done | bytes 278560 | tf_op jit(solution)/shard_map/ppermute | solution.py:1029
  163.6 2.7 %collective-permute-start.9 = (bf16[272,512]{1,0:T(8,128)(2,1)S(1)}, bf16[272,512]{1,0:T(8,128)(2,1)S(1)}, u32[]{:S(2)}, u32[]{:S(2)}) collective-permute-start(bf16[272,512]{1,0:T(8,128)(2,1)S(1)} %add_convert_fusion.8), channel_id=1, source_target_pairs={{0,16},{1,17},{2,18},{3,19},{4,20},{5,21},{6,22},{7,23},{8,24},{9,... | collective-permute-start | bytes 835592 | tf_op jit(solution)/shard_map/ppermute | solution.py:1029
  166.7 11.3 %shard_map.380.small_taps_ref = f32[56,512]{1,0:T(8,128)} custom-call(f32[4,2304,128]{2,1,0:T(8,128)} %get-tuple-element.178.back_in, f32[4,2304,128]{2,1,0:T(8,128)} %get-tuple-element.149.query_in, f32[4,2304,128]{2,1,0:T(8,128)} %get-tuple-element.151.value_in), custom_call_target="tpu_custom_call" | custom-call | flops 15000000512 | bytes 15000000 | tf_op jit(solution)/shard_map/pallas_call | solution.py:1049
  182.6 12.1 %shard_map.381 = (f32[4,1024,128]{2,1,0:T(8,128)}, bf16[80,512]{1,0:T(8,128)(2,1)}) custom-call(bf16[512,1536]{1,0:T(8,128)(2,1)} %qkv_ref.5, bf16[512]{0:T(512)(128)(2,1)} %gain_ref.7, bf16[2048,1536]{1,0:T(8,128)(2,1)} %get-tuple-element.181.projected_in, f32[4,2048,128]{2,1,0:T(8,128)} %get-tuple-element.169.parts_in, ...), custom_call_target="tpu_custom_call" | custom-call | flops 12000000000 | bytes 12000000 | tf_op jit(solution)/shard_map/pallas_call | solution.py:1049
  195.7 2.3 collective-permute-start.19
  199.2 4.2 %shard_map.382 = bf16[1968,512]{1,0:T(8,128)(2,1)} custom-call(bf16[2048,512]{1,0:T(8,128)(2,1)} %get-tuple-element.191.result_ref, f32[2048,128]{1,0:T(8,128)} %get-tuple-element.134.mask_ref.mask_in), custom_call_target="tpu_custom_call" | custom-call | flops 1000000 | bytes 1000 | tf_op jit(solution)/shard_map/pallas_call | solution.py:1049
  203.8 2.4 collective-permute-start.16
  206.2 7.9 %shard_map.383 = bf16[1968,512]{1,0:T(8,128)(2,1)} custom-call(f32[2048,128]{1,0:T(8,128)} %get-tuple-element.134.mask_ref.mask_in, bf16[9,512]{1,0:T(8,128)(2,1)} %cpe_ref.3, f32[4,1024,128]{2,1,0:T(8,128)} %get-tuple-element.182.grad_first_in.first_in, f32[4,1024,128]{2,1,0:T(8,128)} %get-tuple-element.198.second_in), custom_call_target="tpu_custom_call" | custom-call | flops 1000000 | bytes 1000 | tf_op jit(solution)/shard_map/pallas_call | solution.py:1049
  216.6 2.9 %shard_map.384 = (f32[512,512]{1,0:T(8,128)}, f32[512,512]{1,0:T(8,128)}, f32[512]{0:T(512)}) custom-call(s32[3]{0:T(128)} %pad_add_fusion.side_ref, bf16[272,512]{1,0:T(8,128)(2,1)} %copy-done.2, bf16[272,512]{1,0:T(8,128)(2,1)} %copy-done.10, bf16[272,512]{1,0:T(8,128)(2,1)} %copy-done.9, bf16[272,512]{1,0:T(8,128)(2,1)} %copy-done.11), custom_call_target="tpu_custom_call" | custom-call | flops 1000000 | bytes 1000 | tf_op jit(solution)/shard_map/pallas_call | solution.py:1049
  219.8 2.6 %collective-permute-start.27 = (bf16[80,512]{1,0:T(8,128)(2,1)S(1)}, bf16[80,512]{1,0:T(8,128)(2,1)S(1)}, u32[]{:S(2)}, u32[]{:S(2)}) collective-permute-start(bf16[80,512]{1,0:T(8,128)(2,1)S(1)} %add_convert_fusion.15.own_ref), channel_id=1, source_target_pairs={{0,24},{1,25},{2,26},{3,27},{4,28},{5,29},{6,30},{7,31},{8,16},{9,... | collective-permute-start | bytes 245768 | tf_op jit(solution)/shard_map/ppermute | solution.py:1029
  222.4 1.9 collective-permute-start.25
  224.3 4.4 %shard_map.385 = (f32[512,1536]{1,0:T(8,128)}, f32[512,512]{1,0:T(8,128)}, f32[512]{0:T(512)}, f32[512]{0:T(512)}, f32[512]{0:T(512)}, /*index=5*/f32[512]{0:T(512)}, f32[512]{0:T(512)}, f32[512]{0:T(512)}, f32[512]{0:T(512)}) custom-call(s32[3]{0:T(128)} %pad_add_fusion.side_ref, bf16[272,512]{1,0:T(8,128)(2,1)} %copy-done, bf16[272,512]{1,0:T(8,128)(2,1)} %copy-done.6, ...), custom_call_target="tpu_custom_call" | custom-call | flops 1000000 | bytes 1000 | tf_op jit(solution)/shard_map/pallas_call | solution.py:1049
  229.9 1.9 shard_map.386
  (93 shorter events, 21.4 us)
Async XLA Ops:
  7.2 42.7 %all-gather.3.cloned.1.call-start = ((), (), s32[]{:S(2)}) async-start(), calls=%async_computation | async-start | bytes 5324800 | tf_op jit(solution)/shard_map/all_gather | solution.py:1083
  91.2 7.0 %collective-permute-start = (bf16[2,4,272,512]{3,2,1,0:T(8,128)(2,1)}, bf16[2,4,272,512]{3,2,1,0:T(8,128)(2,1)}, u32[]{:S(2)}, u32[]{:S(2)}) collective-permute-start(bf16[2,4,272,512]{3,2,1,0:T(8,128)(2,1)} %get-tuple-element.147), channel_id=1, source_target_pairs={{0,1},{1,0},{2,3},{3,2},{4,5},{5,4},{6,7},{7,6},{8,9},{9,8},{10,11... | collective-permute-start | bytes 6684680 | tf_op jit(solution)/shard_map/ppermute | solution.py:1029
  102.0 39.3 %collective-permute-start.1 = (bf16[2,272,512]{2,1,0:T(8,128)(2,1)}, bf16[2,272,512]{2,1,0:T(8,128)(2,1)}, u32[]{:S(2)}, u32[]{:S(2)}) collective-permute-start(bf16[2,272,512]{2,1,0:T(8,128)(2,1)} %get-tuple-element.158), channel_id=1, source_target_pairs={{0,2},{1,3},{2,0},{3,1},{4,6},{5,7},{6,4},{7,5},{8,10},{9,11},{10,... | collective-permute-start | bytes 1671176 | tf_op jit(solution)/shard_map/ppermute | solution.py:1029
  104.5 36.8 %collective-permute-start.2 = (bf16[2,272,512]{2,1,0:T(8,128)(2,1)S(1)}, bf16[2,272,512]{2,1,0:T(8,128)(2,1)}, u32[]{:S(2)}, u32[]{:S(2)}) collective-permute-start(bf16[2,272,512]{2,1,0:T(8,128)(2,1)S(1)} %get-tuple-element.159), channel_id=1, source_target_pairs={{0,4},{1,5},{2,6},{3,7},{4,0},{5,1},{6,2},{7,3},{8,12},{9,13},{10,... | collective-permute-start | bytes 1671176 | tf_op jit(solution)/shard_map/ppermute | solution.py:1029
  106.0 35.3 %collective-permute-start.3 = (bf16[2,272,512]{2,1,0:T(8,128)(2,1)S(1)}, bf16[2,272,512]{2,1,0:T(8,128)(2,1)}, u32[]{:S(2)}, u32[]{:S(2)}) collective-permute-start(bf16[2,272,512]{2,1,0:T(8,128)(2,1)S(1)} %get-tuple-element.160), channel_id=1, source_target_pairs={{0,6},{1,7},{2,4},{3,5},{4,2},{5,3},{6,0},{7,1},{8,14},{9,15},{10,... | collective-permute-start | bytes 1671176 | tf_op jit(solution)/shard_map/ppermute | solution.py:1029
  144.7 13.5 %collective-permute-start.5 = (bf16[272,512]{1,0:T(8,128)(2,1)S(1)}, bf16[272,512]{1,0:T(8,128)(2,1)}, u32[]{:S(2)}, u32[]{:S(2)}) collective-permute-start(bf16[272,512]{1,0:T(8,128)(2,1)S(1)} %get-tuple-element.173), channel_id=1, source_target_pairs={{0,8},{1,9},{2,10},{3,11},{4,12},{5,13},{6,14},{7,15},{8,0},{9,1},... | collective-permute-start | bytes 835592 | tf_op jit(solution)/shard_map/ppermute | solution.py:1029
  146.7 12.5 %collective-permute-start.6 = (bf16[272,512]{1,0:T(8,128)(2,1)S(1)}, bf16[272,512]{1,0:T(8,128)(2,1)S(1)}, u32[]{:S(2)}, u32[]{:S(2)}) collective-permute-start(bf16[272,512]{1,0:T(8,128)(2,1)S(1)} %get-tuple-element.175), channel_id=1, source_target_pairs={{0,2},{1,3},{2,0},{3,1},{4,6},{5,7},{6,4},{7,5},{8,10},{9,11},{10,... | collective-permute-start | bytes 835592 | tf_op jit(solution)/shard_map/ppermute | solution.py:1029
  148.3 10.9 %collective-permute-start.7 = (bf16[272,512]{1,0:T(8,128)(2,1)S(1)}, bf16[272,512]{1,0:T(8,128)(2,1)}, u32[]{:S(2)}, u32[]{:S(2)}) collective-permute-start(bf16[272,512]{1,0:T(8,128)(2,1)S(1)} %get-tuple-element.176), channel_id=1, source_target_pairs={{0,4},{1,5},{2,6},{3,7},{4,0},{5,1},{6,2},{7,3},{8,12},{9,13},{10,... | collective-permute-start | bytes 835592 | tf_op jit(solution)/shard_map/ppermute | solution.py:1029
  149.8 12.6 %collective-permute-start.8 = (bf16[272,512]{1,0:T(8,128)(2,1)S(1)}, bf16[272,512]{1,0:T(8,128)(2,1)}, u32[]{:S(2)}, u32[]{:S(2)}) collective-permute-start(bf16[272,512]{1,0:T(8,128)(2,1)S(1)} %get-tuple-element.177), channel_id=1, source_target_pairs={{0,6},{1,7},{2,4},{3,5},{4,2},{5,3},{6,0},{7,1},{8,14},{9,15},{10,... | collective-permute-start | bytes 835592 | tf_op jit(solution)/shard_map/ppermute | solution.py:1029
  163.6 14.5 %collective-permute-start.9 = (bf16[272,512]{1,0:T(8,128)(2,1)S(1)}, bf16[272,512]{1,0:T(8,128)(2,1)S(1)}, u32[]{:S(2)}, u32[]{:S(2)}) collective-permute-start(bf16[272,512]{1,0:T(8,128)(2,1)S(1)} %add_convert_fusion.8), channel_id=1, source_target_pairs={{0,16},{1,17},{2,18},{3,19},{4,20},{5,21},{6,22},{7,23},{8,24},{9,... | collective-permute-start | bytes 835592 | tf_op jit(solution)/shard_map/ppermute | solution.py:1029
  166.3 12.7 %collective-permute-start.10 = (bf16[272,512]{1,0:T(8,128)(2,1)S(1)}, bf16[272,512]{1,0:T(8,128)(2,1)S(1)}, u32[]{:S(2)}, u32[]{:S(2)}) collective-permute-start(bf16[272,512]{1,0:T(8,128)(2,1)S(1)} %add_convert_fusion.7), channel_id=1, source_target_pairs={{0,8},{1,9},{2,10},{3,11},{4,12},{5,13},{6,14},{7,15},{8,0},{9,1},... | collective-permute-start | bytes 835592 | tf_op jit(solution)/shard_map/ppermute | solution.py:1029
  179.1 15.8 %collective-permute-start.12 = (bf16[272,512]{1,0:T(8,128)(2,1)S(1)}, bf16[272,512]{1,0:T(8,128)(2,1)S(1)}, u32[]{:S(2)}, u32[]{:S(2)}) collective-permute-start(bf16[272,512]{1,0:T(8,128)(2,1)S(1)} %add_convert_fusion.6.first_ref), channel_id=1, source_target_pairs={{0,4},{1,5},{2,6},{3,7},{4,0},{5,1},{6,2},{7,3},{8,12},{9,13},{10,... | collective-permute-start | bytes 835592 | tf_op jit(solution)/shard_map/ppermute | solution.py:1029
  180.7 14.1 %collective-permute-start.11 = (bf16[272,512]{1,0:T(8,128)(2,1)S(1)}, bf16[272,512]{1,0:T(8,128)(2,1)S(1)}, u32[]{:S(2)}, u32[]{:S(2)}) collective-permute-start(bf16[272,512]{1,0:T(8,128)(2,1)S(1)} %add_convert_fusion.6.first_ref), channel_id=1, source_target_pairs={{0,8},{1,9},{2,10},{3,11},{4,12},{5,13},{6,14},{7,15},{8,0},{9,1},... | collective-permute-start | bytes 835592 | tf_op jit(solution)/shard_map/ppermute | solution.py:1029
  181.4 13.4 %collective-permute-start.13 = (bf16[272,512]{1,0:T(8,128)(2,1)S(1)}, bf16[272,512]{1,0:T(8,128)(2,1)S(1)}, u32[]{:S(2)}, u32[]{:S(2)}) collective-permute-start(bf16[272,512]{1,0:T(8,128)(2,1)S(1)} %add_convert_fusion.5), channel_id=1, source_target_pairs={{0,16},{1,17},{2,18},{3,19},{4,20},{5,21},{6,22},{7,23},{8,24},{9,... | collective-permute-start | bytes 835592 | tf_op jit(solution)/shard_map/ppermute | solution.py:1029
  194.9 8.8 %collective-permute-start.15 = (bf16[272,512]{1,0:T(8,128)(2,1)S(1)}, bf16[272,512]{1,0:T(8,128)(2,1)S(1)}, u32[]{:S(2)}, u32[]{:S(2)}) collective-permute-start(bf16[272,512]{1,0:T(8,128)(2,1)S(1)} %collective-permute-done.11.second_ref), channel_id=1, source_target_pairs={{0,4},{1,5},{2,6},{3,7},{4,0},{5,1},{6,2},{7,3},{8,12},{9,13},{10,... | collective-permute-start | bytes 835592 | tf_op jit(solution)/shard_map/ppermute | solution.py:1029
  195.5 7.8 %collective-permute-start.14 = (bf16[80,512]{1,0:T(8,128)(2,1)}, bf16[80,512]{1,0:T(8,128)(2,1)S(1)}, u32[]{:S(2)}, u32[]{:S(2)}) collective-permute-start(bf16[80,512]{1,0:T(8,128)(2,1)} %get-tuple-element.195), channel_id=1, source_target_pairs={{0,1},{1,0},{2,3},{3,2},{4,5},{5,4},{6,7},{7,6},{8,9},{9,8},{10,11... | collective-permute-start | bytes 245768 | tf_op jit(solution)/shard_map/ppermute | solution.py:1029
  195.7 18.4 %collective-permute-start.19 = (bf16[272,512]{1,0:T(8,128)(2,1)S(1)}, bf16[272,512]{1,0:T(8,128)(2,1)S(1)}, u32[]{:S(2)}, u32[]{:S(2)}) collective-permute-start(bf16[272,512]{1,0:T(8,128)(2,1)S(1)} %add_convert_fusion.4.refs_0_), channel_id=1, source_target_pairs={{0,6},{1,7},{2,4},{3,5},{4,2},{5,3},{6,0},{7,1},{8,14},{9,15},{10,... | collective-permute-start | bytes 835592 | tf_op jit(solution)/shard_map/ppermute | solution.py:1029
  198.0 16.1 %collective-permute-start.18 = (bf16[272,512]{1,0:T(8,128)(2,1)S(1)}, bf16[272,512]{1,0:T(8,128)(2,1)S(1)}, u32[]{:S(2)}, u32[]{:S(2)}) collective-permute-start(bf16[272,512]{1,0:T(8,128)(2,1)S(1)} %add_convert_fusion.4.refs_0_), channel_id=1, source_target_pairs={{0,4},{1,5},{2,6},{3,7},{4,0},{5,1},{6,2},{7,3},{8,12},{9,13},{10,... | collective-permute-start | bytes 835592 | tf_op jit(solution)/shard_map/ppermute | solution.py:1029
  198.6 15.5 %collective-permute-start.17 = (bf16[272,512]{1,0:T(8,128)(2,1)S(1)}, bf16[272,512]{1,0:T(8,128)(2,1)S(1)}, u32[]{:S(2)}, u32[]{:S(2)}) collective-permute-start(bf16[272,512]{1,0:T(8,128)(2,1)S(1)} %add_convert_fusion.4.refs_0_), channel_id=1, source_target_pairs={{0,2},{1,3},{2,0},{3,1},{4,6},{5,7},{6,4},{7,5},{8,10},{9,11},{10,... | collective-permute-start | bytes 835592 | tf_op jit(solution)/shard_map/ppermute | solution.py:1029
  203.8 10.3 %collective-permute-start.16 = (bf16[80,512]{1,0:T(8,128)(2,1)S(1)}, bf16[80,512]{1,0:T(8,128)(2,1)S(1)}, u32[]{:S(2)}, u32[]{:S(2)}) collective-permute-start(bf16[80,512]{1,0:T(8,128)(2,1)S(1)} %add_convert_fusion.17), channel_id=1, source_target_pairs={{0,2},{1,3},{2,0},{3,1},{4,6},{5,7},{6,4},{7,5},{8,10},{9,11},{10,... | collective-permute-start | bytes 245768 | tf_op jit(solution)/shard_map/ppermute | solution.py:1029
  214.1 5.6 %collective-permute-start.21 = (bf16[272,512]{1,0:T(8,128)(2,1)S(1)}, bf16[272,512]{1,0:T(8,128)(2,1)S(1)}, u32[]{:S(2)}, u32[]{:S(2)}) collective-permute-start(bf16[272,512]{1,0:T(8,128)(2,1)S(1)} %add_convert_fusion.4.refs_0_), channel_id=1, source_target_pairs={{0,1},{1,0},{2,3},{3,2},{4,5},{5,4},{6,7},{7,6},{8,9},{9,8},{10,11... | collective-permute-start | bytes 835592 | tf_op jit(solution)/shard_map/ppermute | solution.py:1029
  219.8 8.9 %collective-permute-start.27 = (bf16[80,512]{1,0:T(8,128)(2,1)S(1)}, bf16[80,512]{1,0:T(8,128)(2,1)S(1)}, u32[]{:S(2)}, u32[]{:S(2)}) collective-permute-start(bf16[80,512]{1,0:T(8,128)(2,1)S(1)} %add_convert_fusion.15.own_ref), channel_id=1, source_target_pairs={{0,24},{1,25},{2,26},{3,27},{4,28},{5,29},{6,30},{7,31},{8,16},{9,... | collective-permute-start | bytes 245768 | tf_op jit(solution)/shard_map/ppermute | solution.py:1029
  222.4 6.8 %collective-permute-start.26 = (bf16[80,512]{1,0:T(8,128)(2,1)S(1)}, bf16[80,512]{1,0:T(8,128)(2,1)S(1)}, u32[]{:S(2)}, u32[]{:S(2)}) collective-permute-start(bf16[80,512]{1,0:T(8,128)(2,1)S(1)} %add_convert_fusion.15.own_ref), channel_id=1, source_target_pairs={{0,16},{1,17},{2,18},{3,19},{4,20},{5,21},{6,22},{7,23},{8,24},{9,... | collective-permute-start | bytes 245768 | tf_op jit(solution)/shard_map/ppermute | solution.py:1029
  222.4 6.8 %collective-permute-start.25 = (bf16[80,512]{1,0:T(8,128)(2,1)S(1)}, bf16[80,512]{1,0:T(8,128)(2,1)S(1)}, u32[]{:S(2)}, u32[]{:S(2)}) collective-permute-start(bf16[80,512]{1,0:T(8,128)(2,1)S(1)} %add_convert_fusion.15.own_ref), channel_id=1, source_target_pairs={{0,8},{1,9},{2,10},{3,11},{4,12},{5,13},{6,14},{7,15},{8,0},{9,1},... | collective-permute-start | bytes 245768 | tf_op jit(solution)/shard_map/ppermute | solution.py:1029
  (21 other events, 141.5 us)
Sparse Core Ops, SparseCore 0:
  10.2 37.5 all-gather.2

commit v2 on v1

--- a/solution.py
+++ b/solution.py
@@ -87,14 +87,10 @@
 def fill_mask(side, mask_ref, images):
     mask_ref[SLOT * images :, :] = jnp.zeros_like(mask_ref[SLOT * images :, :])
 
-    def body(slot):
-        row = slot // GRID
-        col = slot - row * GRID
-        inside = (slot == CELLS) | ((row < side) & (col < side))
-        level = jnp.where(inside, 1.0, 0.0).astype(F32)
-        mask_ref[rows_at(slot * images, images), :] = jnp.full((images, LANES), level, F32)
-
-    loop(SLOT, body, unroll=2)
+    inside = [jnp.where(place < side, 1.0, 0.0).astype(F32) for place in range(GRID)]
+    for slot in range(SLOT):
+        level = jnp.float32(1.0) if slot == CELLS else inside[slot // GRID] * inside[slot % GRID]
+        mask_ref[slot * images : (slot + 1) * images, :] = jnp.full((images, LANES), level, F32)
 
 
 def spread(rows_ref, blocks_ref, blocks):
@@ -995,9 +991,7 @@
 
 
 def finish_kernel(side_ref, *refs):
-    pieces, (qkv_out, proj_out), rows = refs[:8], refs[8:10], refs[10:-5]
-    held_ref, small_ref, qkv_ref, proj_ref, sems = refs[-5:]
-    copies = Copies(sems)
+    pieces, (qkv_ref, proj_ref), rows, (held_ref, small_ref) = refs[:8], refs[8:10], refs[10:-2], refs[-2:]
     index = ((side_ref[1] & 1) << 2) | ((side_ref[2] & 1) << 1) | (side_ref[1] >> 1)
     for place, piece in enumerate(pieces):
         held_ref[place ^ index] = piece[...]
@@ -1005,18 +999,14 @@
     for piece in range(8):
         matrix, end = piece // 2, piece % 2
         at = slice(end * PIECE, (end + 1) * PIECE)
-        cols = slice(matrix * channels, (matrix + 1) * channels)
         values = held_ref[piece, 0:PIECE, :].astype(F32)
         if matrix < 3:
-            qkv_ref[at, cols] = values
-            copies.start(qkv_ref.at[at, cols], qkv_out.at[at, cols])
+            qkv_ref[at, matrix * channels : (matrix + 1) * channels] = values
         else:
             proj_ref[at, :] = values
-            copies.start(proj_ref.at[at], proj_out.at[at])
         small_ref[piece * 16 : (piece + 1) * 16, :] = held_ref[piece, PIECE:, :].astype(F32)
     for row, ref in zip(SMALL_ROWS, rows):
         ref[...] = small_ref[row : row + 1, :].reshape(ref.shape)
-    copies.finish()
 
 
 def add(*terms):
@@ -1141,7 +1131,8 @@
         part = slice(2 * end, 2 * end + 2)
         return add(fc_keep[side, part], fc_far[side, part])
 
-    back, fc_y, fc_x, fc_yx, fc_own = together(back, half_of(1, 0), half_of(0, 1), half_of(1, 1), half_of(0, 0))
+    back, fc_y, fc_x, fc_yx = together(back, half_of(1, 0), half_of(0, 1), half_of(1, 1))
+    fc_core = fc_far
     fc_far = exchange(fc_y, 0, 2), exchange(fc_x, 1, 0), exchange(fc_yx, 1, 2)
     total_keep, total_send, projected = call(
         mix_kernel,
@@ -1164,7 +1155,7 @@
     fc_bits = [bit for bit in bits if bit > 2]
 
     def end_of(end):
-        return add(fc_own[end], *(far[end] for far in fc_far))
+        return add(fc_keep[0, end], fc_core[0, end], *(far[end] for far in fc_far))
 
     fc_other, fc_own = end_of(1), end_of(0)
     sums = [add(total_keep[piece], total_far[piece]) for piece in range(4)]
@@ -1249,11 +1240,8 @@
     row = shape((channels,), F32)
     grad_qkv, grad_proj, query_sums, value_sums, crpe_sums, proj_sums, gain_two, shift_two, fc2_sums = call(
         finish_kernel,
-        [Held(shape((channels, 3 * channels), F32)), Held(shape((channels, channels), F32))] + [row] * len(SMALL_ROWS),
-        [
-            ((8, PIECE + 16, channels), BF16), ((128, channels), F32),
-            ((channels, 3 * channels), F32), ((channels, channels), F32), 8,
-        ],
+        [shape((channels, 3 * channels), F32), shape((channels, channels), F32)] + [row] * len(SMALL_ROWS),
+        [((8, PIECE + 16, channels), BF16), ((128, channels), F32)],
         1_000_000,
         scalars, *total_pieces,
     )

time: 243 us -> 243 us (level)
    convert_element_type x10 -> x11, other arithmetic: 6.56 us -> 8.01 us  [add(): return sum((term.astype(F32) for term in terms)).astype(BF16)]
where the time goes in v2:
time: 243 us; the launch traced here: 239 us
  Pallas kernels  176 us (72%)
  starting transfers between devices  30.2 us (12%)
  between operations  15.3 us (6%)
  other arithmetic  8.6 us (4%)
  waiting for transfers between devices  7.13 us (3%)
    pallas_call x14, Pallas kernels, call(): pl.pallas_call(body, out_shape=plain(outs), in_specs=[place(value) for va...  176 us
    ppermute x28, starting transfers between devices, exchange(): lax.ppermute(values, ('dp', 'blk'), [(at, at ^ flip) for at in range(part...  30.2 us
    convert_element_type x11, other arithmetic, add(): return sum((term.astype(F32) for term in terms)).astype(BF16)  8.01 us
    ppermute x28, waiting for transfers between devices, exchange(): lax.ppermute(values, ('dp', 'blk'), [(at, at ^ flip) for at in range(part...  7.09 us
  transfers between devices with their start and end apart: 29, of which 6 were waited for; matrix products, arithmetic and copies ran while one was open for 1% of the time, Pallas kernels for 55%

profile of v2, /device:TPU:0, one launch (start us, length us, event | category | flops | bytes accessed | tf_op | source)
XLA Modules:
  0.0 238.5 jit_solution(6938380407200767941)
XLA Ops:
  7.2 2.3 shard_map.375
  10.8 32.5 %shard_map.373 = (f32[56,512]{1,0:T(8,128)}, f32[2048,128]{1,0:T(8,128)}, f32[4,2048,128]{2,1,0:T(8,128)}, f32[4,2048,128]{2,1,0:T(8,128)}, f32[2048,128]{1,0:T(...) custom-call(s32[3]{0:T(128)} %pad_add_fusion.side_ref, ...), custom_call_target="tpu_custom_call" | custom-call | flops 40000000000 | bytes 40000000 | tf_op jit(solution)/shard_map/pallas_call | solution.py:1039
  43.3 5.8 %shard_map.374 = (bf16[2048,512]{1,0:T(8,128)(2,1)}, bf16[512,2048]{1,0:T(8,128)(2,1)}, f32[8,512]{1,0:T(8,128)}) custom-call(bf16[1968,512]{1,0:T(8,128)(2,1)} %cot_ref.1, f32[2048,128]{1,0:T(8,128)} %get-tuple-element.133.mask_ref.mask_in), custom_call_target="tpu_custom_call" | custom-call | flops 6000000000 | bytes 6000000 | tf_op jit(solution)/shard_map/pallas_call | solution.py:1039
  49.1 41.3 %shard_map.376 = (bf16[2048,512]{1,0:T(8,128)(2,1)}, f32[4,2048,128]{2,1,0:T(8,128)}, bf16[2,4,272,512]{3,2,1,0:T(8,128)(2,1)}, bf16[2,4,272,512]{3,2,1,0:T(8,128)(2,1)}, f32[8,512]{1,0:T(8,128)}) custom-call(s32[3]{0:T(128)} %pad_add_fusion.side_ref, f32[8,512]{1,0:T(8,128)} %get-tuple-element.134.bias_sums_ref, ...), custom_call_target="tpu_custom_call" | custom-call | flops 60000002048 | bytes 60000000 | tf_op jit(solution)/shard_map/pallas_call | solution.py:1039
  90.9 6.5 %shard_map.377 = (f32[4,2304,128]{2,1,0:T(8,128)}, bf16[512,512]{1,0:T(8,128)(2,1)}, f32[8,512]{1,0:T(8,128)}) custom-call(bf16[512,512]{1,0:T(8,128)(2,1)} %proj_ref.3, f32[4,2048,128]{2,1,0:T(8,128)} %get-tuple-element.139.grad_in, bf16[512,2048]{1,0:T(8,128)(2,1)} %get-tuple-element.140.attended_t_in), custom_call_target="tpu_custom_call" | custom-call | flops 10000000000 | bytes 10000000 | tf_op jit(solution)/shard_map/pallas_call | solution.py:1039
  97.4 3.4 %fusion.2 = (bf16[2,272,512]{2,1,0:T(8,128)(2,1)}, bf16[2,272,512]{2,1,0:T(8,128)(2,1)}, bf16[2,272,512]{2,1,0:T(8,128)(2,1)}) fusion(bf16[2,4,272,512]{3,2,1,0:T(8,128)(2,1)} %collective-permute-done, bf16[2,4,272,512]{3,2,1,0:T(8,128)(2,1)} %get-tuple-element.145), kind=kLoop, calls=%fused_computation.5 | loop fusion | flops 3342336 | bytes 5013504 | tf_op jit(solution)/shard_map/convert_element_type | solution.py:1013
  100.8 2.5 %collective-permute-start.1 = (bf16[2,272,512]{2,1,0:T(8,128)(2,1)}, bf16[2,272,512]{2,1,0:T(8,128)(2,1)S(1)}, u32[]{:S(2)}, u32[]{:S(2)}) collective-permute-start(bf16[2,272,512]{2,1,0:T(8,128)(2,1)} %get-tuple-element.157), channel_id=1, source_target_pairs={{0,2},{1,3},{2,0},{3,1},{4,6},{5,7},{6,4},{7,5},{8,10},{9,11},{10,... | collective-permute-start | bytes 1671176 | tf_op jit(solution)/shard_map/ppermute | solution.py:1019
  104.8 35.2 %shard_map.378 = (bf16[4,272,512]{2,1,0:T(8,128)(2,1)}, bf16[4,272,512]{2,1,0:T(8,128)(2,1)}, bf16[2048,1536]{1,0:T(8,128)(2,1)}) custom-call(s32[3]{0:T(128)} %pad_add_fusion.side_ref, f32[8,512]{1,0:T(8,128)} %get-tuple-element.138.small_mlp_ref, f32[8,512]{1,0:T(8,128)} %get-tuple-element.141.small_branch_ref, f32[56,512]{1,0:T(8,128)} %get-tuple-element.142.crpe_ref, ...), custom_call_target="tpu_custom_call" | custom-call | flops 49999998976 | bytes 50000000 | tf_op jit(solution)/shard_map/pallas_call | solution.py:1039
  140.9 1.7 fusion.3
  144.2 2.1 collective-permute-start.5
  149.8 7.9 %shard_map.379 = (f32[4,1024,128]{2,1,0:T(8,128)}, f32[8,512]{1,0:T(8,128)}) custom-call(bf16[512,1536]{1,0:T(8,128)(2,1)} %qkv_ref.5, bf16[512]{0:T(512)(128)(2,1)} %gain_ref.7, bf16[2048,1536]{1,0:T(8,128)(2,1)} %get-tuple-element.179.projected_in, f32[4,2048,128]{2,1,0:T(8,128)} %get-tuple-element.167.parts_in, ...), custom_call_target="tpu_custom_call" | custom-call | flops 8000000000 | bytes 8000000 | tf_op jit(solution)/shard_map/pallas_call | solution.py:1039
  158.8 3.2 %collective-permute-done.8 = bf16[272,512]{1,0:T(8,128)(2,1)} collective-permute-done((bf16[272,512]{1,0:T(8,128)(2,1)S(1)}, bf16[272,512]{1,0:T(8,128)(2,1)}, u32[]{:S(2)}, u32[]{:S(2)}) %collective-permute-start.8) | collective-permute-done | bytes 278560 | tf_op jit(solution)/shard_map/ppermute | solution.py:1019
  163.3 2.6 %collective-permute-start.9 = (bf16[272,512]{1,0:T(8,128)(2,1)S(1)}, bf16[272,512]{1,0:T(8,128)(2,1)S(1)}, u32[]{:S(2)}, u32[]{:S(2)}) collective-permute-start(bf16[272,512]{1,0:T(8,128)(2,1)S(1)} %add_convert_fusion.7), channel_id=1, source_target_pairs={{0,16},{1,17},{2,18},{3,19},{4,20},{5,21},{6,22},{7,23},{8,24},{9,... | collective-permute-start | bytes 835592 | tf_op jit(solution)/shard_map/ppermute | solution.py:1019
  166.4 11.3 %shard_map.380.small_taps_ref = f32[56,512]{1,0:T(8,128)} custom-call(f32[4,2304,128]{2,1,0:T(8,128)} %get-tuple-element.176.back_in, f32[4,2304,128]{2,1,0:T(8,128)} %get-tuple-element.148.query_in, f32[4,2304,128]{2,1,0:T(8,128)} %get-tuple-element.150.value_in), custom_call_target="tpu_custom_call" | custom-call | flops 15000000512 | bytes 15000000 | tf_op jit(solution)/shard_map/pallas_call | solution.py:1039
  182.2 12.2 %shard_map.381 = (f32[4,1024,128]{2,1,0:T(8,128)}, bf16[80,512]{1,0:T(8,128)(2,1)}) custom-call(bf16[512,1536]{1,0:T(8,128)(2,1)} %qkv_ref.5, bf16[512]{0:T(512)(128)(2,1)} %gain_ref.7, bf16[2048,1536]{1,0:T(8,128)(2,1)} %get-tuple-element.179.projected_in, f32[4,2048,128]{2,1,0:T(8,128)} %get-tuple-element.167.parts_in, ...), custom_call_target="tpu_custom_call" | custom-call | flops 12000000000 | bytes 12000000 | tf_op jit(solution)/shard_map/pallas_call | solution.py:1039
  195.3 2.3 collective-permute-start.19
  198.8 4.2 %shard_map.382 = bf16[1968,512]{1,0:T(8,128)(2,1)} custom-call(bf16[2048,512]{1,0:T(8,128)(2,1)} %get-tuple-element.189.result_ref, f32[2048,128]{1,0:T(8,128)} %get-tuple-element.133.mask_ref.mask_in), custom_call_target="tpu_custom_call" | custom-call | flops 1000000 | bytes 1000 | tf_op jit(solution)/shard_map/pallas_call | solution.py:1039
  203.4 2.4 %collective-permute-start.16 = (bf16[80,512]{1,0:T(8,128)(2,1)S(1)}, bf16[80,512]{1,0:T(8,128)(2,1)S(1)}, u32[]{:S(2)}, u32[]{:S(2)}) collective-permute-start(bf16[80,512]{1,0:T(8,128)(2,1)S(1)} %add_convert_fusion.14), channel_id=1, source_target_pairs={{0,2},{1,3},{2,0},{3,1},{4,6},{5,7},{6,4},{7,5},{8,10},{9,11},{10,... | collective-permute-start | bytes 245768 | tf_op jit(solution)/shard_map/ppermute | solution.py:1019
  205.9 7.9 %shard_map.383 = bf16[1968,512]{1,0:T(8,128)(2,1)} custom-call(f32[2048,128]{1,0:T(8,128)} %get-tuple-element.133.mask_ref.mask_in, bf16[9,512]{1,0:T(8,128)(2,1)} %cpe_ref.3, f32[4,1024,128]{2,1,0:T(8,128)} %get-tuple-element.180.grad_first_in.first_in, f32[4,1024,128]{2,1,0:T(8,128)} %get-tuple-element.196.second_in), custom_call_target="tpu_custom_call" | custom-call | flops 1000000 | bytes 1000 | tf_op jit(solution)/shard_map/pallas_call | solution.py:1039
  216.2 2.9 %shard_map.384 = (f32[512,512]{1,0:T(8,128)}, f32[512,512]{1,0:T(8,128)}, f32[512]{0:T(512)}) custom-call(s32[3]{0:T(128)} %pad_add_fusion.side_ref, bf16[272,512]{1,0:T(8,128)(2,1)} %copy-done.2, bf16[272,512]{1,0:T(8,128)(2,1)} %copy-done.11, bf16[272,512]{1,0:T(8,128)(2,1)} %copy-done.10, bf16[272,512]{1,0:T(8,128)(2,1)} %copy-done.12), custom_call_target="tpu_custom_call" | custom-call | flops 1000000 | bytes 1000 | tf_op jit(solution)/shard_map/pallas_call | solution.py:1039
  219.5 2.6 %collective-permute-start.27 = (bf16[80,512]{1,0:T(8,128)(2,1)S(1)}, bf16[80,512]{1,0:T(8,128)(2,1)S(1)}, u32[]{:S(2)}, u32[]{:S(2)}) collective-permute-start(bf16[80,512]{1,0:T(8,128)(2,1)S(1)} %add_convert_fusion.12.own_ref), channel_id=1, source_target_pairs={{0,24},{1,25},{2,26},{3,27},{4,28},{5,29},{6,30},{7,31},{8,16},{9,... | collective-permute-start | bytes 245768 | tf_op jit(solution)/shard_map/ppermute | solution.py:1019
  222.1 1.9 collective-permute-start.25
  224.0 3.8 %shard_map.385 = (f32[512,1536]{1,0:T(8,128)}, f32[512,512]{1,0:T(8,128)}, f32[512]{0:T(512)}, f32[512]{0:T(512)}, f32[512]{0:T(512)}, /*index=5*/f32[512]{0:T(512)}, f32[512]{0:T(512)}, f32[512]{0:T(512)}, f32[512]{0:T(512)}) custom-call(s32[3]{0:T(128)} %pad_add_fusion.side_ref, bf16[272,512]{1,0:T(8,128)(2,1)} %copy-done, bf16[272,512]{1,0:T(8,128)(2,1)} %copy-done.7, ...), custom_call_target="tpu_custom_call" | custom-call | flops 1000000 | bytes 1000 | tf_op jit(solution)/shard_map/pallas_call | solution.py:1039
  229.6 1.9 shard_map.386
  (95 shorter events, 22.8 us)
Async XLA Ops:
  7.2 41.9 %all-gather.3.cloned.1.call-start = ((), (), s32[]{:S(2)}) async-start(), calls=%async_computation | async-start | bytes 5324800 | tf_op jit(solution)/shard_map/all_gather | solution.py:1073
  90.4 7.0 %collective-permute-start = (bf16[2,4,272,512]{3,2,1,0:T(8,128)(2,1)}, bf16[2,4,272,512]{3,2,1,0:T(8,128)(2,1)}, u32[]{:S(2)}, u32[]{:S(2)}) collective-permute-start(bf16[2,4,272,512]{3,2,1,0:T(8,128)(2,1)} %get-tuple-element.146), channel_id=1, source_target_pairs={{0,1},{1,0},{2,3},{3,2},{4,5},{5,4},{6,7},{7,6},{8,9},{9,8},{10,11... | collective-permute-start | bytes 6684680 | tf_op jit(solution)/shard_map/ppermute | solution.py:1019
  100.8 39.3 %collective-permute-start.1 = (bf16[2,272,512]{2,1,0:T(8,128)(2,1)}, bf16[2,272,512]{2,1,0:T(8,128)(2,1)S(1)}, u32[]{:S(2)}, u32[]{:S(2)}) collective-permute-start(bf16[2,272,512]{2,1,0:T(8,128)(2,1)} %get-tuple-element.157), channel_id=1, source_target_pairs={{0,2},{1,3},{2,0},{3,1},{4,6},{5,7},{6,4},{7,5},{8,10},{9,11},{10,... | collective-permute-start | bytes 1671176 | tf_op jit(solution)/shard_map/ppermute | solution.py:1019
  103.3 36.7 %collective-permute-start.2 = (bf16[2,272,512]{2,1,0:T(8,128)(2,1)}, bf16[2,272,512]{2,1,0:T(8,128)(2,1)S(1)}, u32[]{:S(2)}, u32[]{:S(2)}) collective-permute-start(bf16[2,272,512]{2,1,0:T(8,128)(2,1)} %get-tuple-element.158), channel_id=1, source_target_pairs={{0,4},{1,5},{2,6},{3,7},{4,0},{5,1},{6,2},{7,3},{8,12},{9,13},{10,... | collective-permute-start | bytes 1671176 | tf_op jit(solution)/shard_map/ppermute | solution.py:1019
  104.8 35.3 %collective-permute-start.3 = (bf16[2,272,512]{2,1,0:T(8,128)(2,1)}, bf16[2,272,512]{2,1,0:T(8,128)(2,1)S(1)}, u32[]{:S(2)}, u32[]{:S(2)}) collective-permute-start(bf16[2,272,512]{2,1,0:T(8,128)(2,1)} %get-tuple-element.159), channel_id=1, source_target_pairs={{0,6},{1,7},{2,4},{3,5},{4,2},{5,3},{6,0},{7,1},{8,14},{9,15},{10,... | collective-permute-start | bytes 1671176 | tf_op jit(solution)/shard_map/ppermute | solution.py:1019
  144.2 13.6 %collective-permute-start.5 = (bf16[272,512]{1,0:T(8,128)(2,1)S(1)}, bf16[272,512]{1,0:T(8,128)(2,1)}, u32[]{:S(2)}, u32[]{:S(2)}) collective-permute-start(bf16[272,512]{1,0:T(8,128)(2,1)S(1)} %get-tuple-element.171), channel_id=1, source_target_pairs={{0,8},{1,9},{2,10},{3,11},{4,12},{5,13},{6,14},{7,15},{8,0},{9,1},... | collective-permute-start | bytes 835592 | tf_op jit(solution)/shard_map/ppermute | solution.py:1019
  146.3 12.5 %collective-permute-start.6 = (bf16[272,512]{1,0:T(8,128)(2,1)S(1)}, bf16[272,512]{1,0:T(8,128)(2,1)}, u32[]{:S(2)}, u32[]{:S(2)}) collective-permute-start(bf16[272,512]{1,0:T(8,128)(2,1)S(1)} %get-tuple-element.173), channel_id=1, source_target_pairs={{0,2},{1,3},{2,0},{3,1},{4,6},{5,7},{6,4},{7,5},{8,10},{9,11},{10,... | collective-permute-start | bytes 835592 | tf_op jit(solution)/shard_map/ppermute | solution.py:1019
  147.9 11.0 %collective-permute-start.7 = (bf16[272,512]{1,0:T(8,128)(2,1)S(1)}, bf16[272,512]{1,0:T(8,128)(2,1)}, u32[]{:S(2)}, u32[]{:S(2)}) collective-permute-start(bf16[272,512]{1,0:T(8,128)(2,1)S(1)} %get-tuple-element.174), channel_id=1, source_target_pairs={{0,4},{1,5},{2,6},{3,7},{4,0},{5,1},{6,2},{7,3},{8,12},{9,13},{10,... | collective-permute-start | bytes 835592 | tf_op jit(solution)/shard_map/ppermute | solution.py:1019
  149.4 12.6 %collective-permute-start.8 = (bf16[272,512]{1,0:T(8,128)(2,1)S(1)}, bf16[272,512]{1,0:T(8,128)(2,1)}, u32[]{:S(2)}, u32[]{:S(2)}) collective-permute-start(bf16[272,512]{1,0:T(8,128)(2,1)S(1)} %get-tuple-element.175), channel_id=1, source_target_pairs={{0,6},{1,7},{2,4},{3,5},{4,2},{5,3},{6,0},{7,1},{8,14},{9,15},{10,... | collective-permute-start | bytes 835592 | tf_op jit(solution)/shard_map/ppermute | solution.py:1019
  163.3 14.4 %collective-permute-start.9 = (bf16[272,512]{1,0:T(8,128)(2,1)S(1)}, bf16[272,512]{1,0:T(8,128)(2,1)S(1)}, u32[]{:S(2)}, u32[]{:S(2)}) collective-permute-start(bf16[272,512]{1,0:T(8,128)(2,1)S(1)} %add_convert_fusion.7), channel_id=1, source_target_pairs={{0,16},{1,17},{2,18},{3,19},{4,20},{5,21},{6,22},{7,23},{8,24},{9,... | collective-permute-start | bytes 835592 | tf_op jit(solution)/shard_map/ppermute | solution.py:1019
  165.9 12.7 %collective-permute-start.10 = (bf16[272,512]{1,0:T(8,128)(2,1)S(1)}, bf16[272,512]{1,0:T(8,128)(2,1)S(1)}, u32[]{:S(2)}, u32[]{:S(2)}) collective-permute-start(bf16[272,512]{1,0:T(8,128)(2,1)S(1)} %add_convert_fusion.6), channel_id=1, source_target_pairs={{0,8},{1,9},{2,10},{3,11},{4,12},{5,13},{6,14},{7,15},{8,0},{9,1},... | collective-permute-start | bytes 835592 | tf_op jit(solution)/shard_map/ppermute | solution.py:1019
  178.7 15.8 %collective-permute-start.12 = (bf16[272,512]{1,0:T(8,128)(2,1)S(1)}, bf16[272,512]{1,0:T(8,128)(2,1)S(1)}, u32[]{:S(2)}, u32[]{:S(2)}) collective-permute-start(bf16[272,512]{1,0:T(8,128)(2,1)S(1)} %add_convert_fusion.5.first_ref), channel_id=1, source_target_pairs={{0,4},{1,5},{2,6},{3,7},{4,0},{5,1},{6,2},{7,3},{8,12},{9,13},{10,... | collective-permute-start | bytes 835592 | tf_op jit(solution)/shard_map/ppermute | solution.py:1019
  180.4 14.2 %collective-permute-start.11 = (bf16[272,512]{1,0:T(8,128)(2,1)S(1)}, bf16[272,512]{1,0:T(8,128)(2,1)S(1)}, u32[]{:S(2)}, u32[]{:S(2)}) collective-permute-start(bf16[272,512]{1,0:T(8,128)(2,1)S(1)} %add_convert_fusion.5.first_ref), channel_id=1, source_target_pairs={{0,8},{1,9},{2,10},{3,11},{4,12},{5,13},{6,14},{7,15},{8,0},{9,1},... | collective-permute-start | bytes 835592 | tf_op jit(solution)/shard_map/ppermute | solution.py:1019
  181.0 13.4 %collective-permute-start.13 = (bf16[272,512]{1,0:T(8,128)(2,1)S(1)}, bf16[272,512]{1,0:T(8,128)(2,1)S(1)}, u32[]{:S(2)}, u32[]{:S(2)}) collective-permute-start(bf16[272,512]{1,0:T(8,128)(2,1)S(1)} %add_convert_fusion.4), channel_id=1, source_target_pairs={{0,16},{1,17},{2,18},{3,19},{4,20},{5,21},{6,22},{7,23},{8,24},{9,... | collective-permute-start | bytes 835592 | tf_op jit(solution)/shard_map/ppermute | solution.py:1019
  194.6 8.8 %collective-permute-start.15 = (bf16[272,512]{1,0:T(8,128)(2,1)S(1)}, bf16[272,512]{1,0:T(8,128)(2,1)S(1)}, u32[]{:S(2)}, u32[]{:S(2)}) collective-permute-start(bf16[272,512]{1,0:T(8,128)(2,1)S(1)} %collective-permute-done.11.second_ref), channel_id=1, source_target_pairs={{0,4},{1,5},{2,6},{3,7},{4,0},{5,1},{6,2},{7,3},{8,12},{9,13},{10,... | collective-permute-start | bytes 835592 | tf_op jit(solution)/shard_map/ppermute | solution.py:1019
  195.1 7.8 %collective-permute-start.14 = (bf16[80,512]{1,0:T(8,128)(2,1)}, bf16[80,512]{1,0:T(8,128)(2,1)S(1)}, u32[]{:S(2)}, u32[]{:S(2)}) collective-permute-start(bf16[80,512]{1,0:T(8,128)(2,1)} %get-tuple-element.193), channel_id=1, source_target_pairs={{0,1},{1,0},{2,3},{3,2},{4,5},{5,4},{6,7},{7,6},{8,9},{9,8},{10,11... | collective-permute-start | bytes 245768 | tf_op jit(solution)/shard_map/ppermute | solution.py:1019
  195.3 18.4 %collective-permute-start.19 = (bf16[272,512]{1,0:T(8,128)(2,1)S(1)}, bf16[272,512]{1,0:T(8,128)(2,1)S(1)}, u32[]{:S(2)}, u32[]{:S(2)}) collective-permute-start(bf16[272,512]{1,0:T(8,128)(2,1)S(1)} %add_convert_fusion.3.refs_0_), channel_id=1, source_target_pairs={{0,6},{1,7},{2,4},{3,5},{4,2},{5,3},{6,0},{7,1},{8,14},{9,15},{10,... | collective-permute-start | bytes 835592 | tf_op jit(solution)/shard_map/ppermute | solution.py:1019
  197.6 16.1 %collective-permute-start.18 = (bf16[272,512]{1,0:T(8,128)(2,1)S(1)}, bf16[272,512]{1,0:T(8,128)(2,1)S(1)}, u32[]{:S(2)}, u32[]{:S(2)}) collective-permute-start(bf16[272,512]{1,0:T(8,128)(2,1)S(1)} %add_convert_fusion.3.refs_0_), channel_id=1, source_target_pairs={{0,4},{1,5},{2,6},{3,7},{4,0},{5,1},{6,2},{7,3},{8,12},{9,13},{10,... | collective-permute-start | bytes 835592 | tf_op jit(solution)/shard_map/ppermute | solution.py:1019
  198.3 15.5 %collective-permute-start.17 = (bf16[272,512]{1,0:T(8,128)(2,1)S(1)}, bf16[272,512]{1,0:T(8,128)(2,1)S(1)}, u32[]{:S(2)}, u32[]{:S(2)}) collective-permute-start(bf16[272,512]{1,0:T(8,128)(2,1)S(1)} %add_convert_fusion.3.refs_0_), channel_id=1, source_target_pairs={{0,2},{1,3},{2,0},{3,1},{4,6},{5,7},{6,4},{7,5},{8,10},{9,11},{10,... | collective-permute-start | bytes 835592 | tf_op jit(solution)/shard_map/ppermute | solution.py:1019
  203.4 10.4 %collective-permute-start.16 = (bf16[80,512]{1,0:T(8,128)(2,1)S(1)}, bf16[80,512]{1,0:T(8,128)(2,1)S(1)}, u32[]{:S(2)}, u32[]{:S(2)}) collective-permute-start(bf16[80,512]{1,0:T(8,128)(2,1)S(1)} %add_convert_fusion.14), channel_id=1, source_target_pairs={{0,2},{1,3},{2,0},{3,1},{4,6},{5,7},{6,4},{7,5},{8,10},{9,11},{10,... | collective-permute-start | bytes 245768 | tf_op jit(solution)/shard_map/ppermute | solution.py:1019
  213.8 5.6 %collective-permute-start.21 = (bf16[272,512]{1,0:T(8,128)(2,1)S(1)}, bf16[272,512]{1,0:T(8,128)(2,1)S(1)}, u32[]{:S(2)}, u32[]{:S(2)}) collective-permute-start(bf16[272,512]{1,0:T(8,128)(2,1)S(1)} %add_convert_fusion.3.refs_0_), channel_id=1, source_target_pairs={{0,1},{1,0},{2,3},{3,2},{4,5},{5,4},{6,7},{7,6},{8,9},{9,8},{10,11... | collective-permute-start | bytes 835592 | tf_op jit(solution)/shard_map/ppermute | solution.py:1019
  219.5 8.3 %collective-permute-start.27 = (bf16[80,512]{1,0:T(8,128)(2,1)S(1)}, bf16[80,512]{1,0:T(8,128)(2,1)S(1)}, u32[]{:S(2)}, u32[]{:S(2)}) collective-permute-start(bf16[80,512]{1,0:T(8,128)(2,1)S(1)} %add_convert_fusion.12.own_ref), channel_id=1, source_target_pairs={{0,24},{1,25},{2,26},{3,27},{4,28},{5,29},{6,30},{7,31},{8,16},{9,... | collective-permute-start | bytes 245768 | tf_op jit(solution)/shard_map/ppermute | solution.py:1019
  222.1 6.8 %collective-permute-start.26 = (bf16[80,512]{1,0:T(8,128)(2,1)S(1)}, bf16[80,512]{1,0:T(8,128)(2,1)S(1)}, u32[]{:S(2)}, u32[]{:S(2)}) collective-permute-start(bf16[80,512]{1,0:T(8,128)(2,1)S(1)} %add_convert_fusion.12.own_ref), channel_id=1, source_target_pairs={{0,16},{1,17},{2,18},{3,19},{4,20},{5,21},{6,22},{7,23},{8,24},{9,... | collective-permute-start | bytes 245768 | tf_op jit(solution)/shard_map/ppermute | solution.py:1019
  222.1 6.8 %collective-permute-start.25 = (bf16[80,512]{1,0:T(8,128)(2,1)S(1)}, bf16[80,512]{1,0:T(8,128)(2,1)S(1)}, u32[]{:S(2)}, u32[]{:S(2)}) collective-permute-start(bf16[80,512]{1,0:T(8,128)(2,1)S(1)} %add_convert_fusion.12.own_ref), channel_id=1, source_target_pairs={{0,8},{1,9},{2,10},{3,11},{4,12},{5,13},{6,14},{7,15},{8,0},{9,1},... | collective-permute-start | bytes 245768 | tf_op jit(solution)/shard_map/ppermute | solution.py:1019
  (22 other events, 143.5 us)
Sparse Core Ops, SparseCore 0:
  10.2 37.5 all-gather.2
